TPU v7x, 256 devices: a whole 4x4x8 slice. The times are simulated.
256 devices in a mesh: span: 16 (over y, x), chord: 8 (over z), wall: 2 (over core).
Axes of the slice: x: 4, y: 4, z: 8, core: 2. Of those that a mesh axis runs over, the one named last changes fastest.
Arguments:
- adjoint_start: float32 [5, 125, 32768], P(None, None, ('span', 'chord', 'wall')), may hold values from -6 to 6
- objective_grad: float32 [5, 125, 32768], P(None, None, ('span', 'chord', 'wall')), may hold values from -30 to 30
- conserved: float32 [5, 125, 32768], P(None, None, ('span', 'chord', 'wall'))
- metric_scale: float32 [32768], P(('span', 'chord', 'wall')), may hold values from 0.25 to 1
- time_step: float32 [32768], P(('span', 'chord', 'wall')), may hold values from 0.02 to 0.06
- viscosity: float32 [32768], P(('span', 'chord', 'wall')), may hold values from 0.05 to 0.4
- face_penalty: float32 [6, 32768], P(None, ('span', 'chord', 'wall')), may hold values from 2 to 8
- face_neighbor: int32 [6, 32768], P(None, ('span', 'chord', 'wall')), may hold values from -1 to 32767, as said below
- neighbor_face: int32 [6, 32768], P(None, ('span', 'chord', 'wall')), may hold values from 0 to 5
- face_orient: int32 [6, 32768], P(None, ('span', 'chord', 'wall')), may hold values from 0 to 3
- wall_elem: int32 [32768], P(('span', 'chord', 'wall')), may hold values from 0 to 127
- wall_face: int32 [32768], P(('span', 'chord', 'wall')), may hold values from 0 to 5
- wall_partial: float32 [3, 125, 32768], P(None, None, ('span', 'chord', 'wall')), may hold values from -0.5 to 0.5
- owner_device: int32 [32768, 1], P(('span', 'chord', 'wall')), may hold values from 0 to 255; in each aligned block of 128 rows (0 to 127, 128 to 255, ...) at most 2 rows name the same one
- owner_slot: int32 [32768], P(('span', 'chord', 'wall')), may hold values from 0 to 127
Outputs:
- adjoint: float32 [5, 125, 32768], P(None, None, ('span', 'chord', 'wall'))
- design_sens: float32 [3, 32768], P(None, ('span', 'chord', 'wall'))
Inputs may be any that keep to these rules, and one draw needn't show every extreme that they name: `face_neighbor`: an element of partition p (p = element // 128, with partition p = (s * 8 + c) * 2 + w) has across each face either -1, an element of p, or an element of a partition whose (s, c, w) differs from p's by one in exactly one of the three. Over all faces of the elements of one partition, at most 64 name elements of one given other partition, and exactly 64 for every partition beside it. `owner_device`: among the wall faces of one partition, no owner partition is named more than 2 times, a bound that some block reaches.
All inputs are finite; a program needn't handle non-finite values.
Results may differ from a plain program's by a relative error of at most 0.0003.
Values sent between devices are 32-bit elements; how exact they have to be, the bound alone decides.
A program may use at most 320 MiB of HBM per device.

v0:
```python
import functools
import math

import jax
import jax.numpy as jnp
import numpy as np
from jax import lax
from jax.sharding import PartitionSpec as P

DES_DEV = 128


GAMMA = 1.4


def passed_along(block, axis, distance):
    devices = range(lax.axis_size(axis))
    route = [(i - distance, i) for i in devices if i - distance in devices]
    return lax.ppermute(block, axis, route)


def derivative_table():
    points = [-1.0, -math.sqrt(3.0 / 7.0), 0.0, math.sqrt(3.0 / 7.0), 1.0]
    barycentric = []
    for i in range(5):
        product_value = 1.0
        for j in range(5):
            if j != i:
                product_value = product_value * (points[i] - points[j])
        barycentric.append(1.0 / product_value)
    matrix_values = np.zeros((5, 5))
    for i in range(5):
        for j in range(5):
            if j != i:
                matrix_values[i, j] = barycentric[j] / barycentric[i] / (points[i] - points[j])
        matrix_values[i, i] = -np.sum(matrix_values[i])
    return matrix_values


def sweep(field_five, axis_dir, transposed):
    matrix = jnp.asarray(derivative_table(), dtype=jnp.float32)
    contracted = 0 if transposed else 1
    contracted_field = jnp.tensordot(
        matrix, field_five, axes=((contracted,), (1 + axis_dir,)), precision=lax.Precision.HIGHEST
    )
    return jnp.moveaxis(contracted_field, 0, 1 + axis_dir)


def axis_flux(axis_dir, conserved):
    density = conserved[0]
    momentum = [conserved[1], conserved[2], conserved[3]]
    kinetic = (
        0.5
        * (momentum[0] * momentum[0] + momentum[1] * momentum[1] + momentum[2] * momentum[2])
        / density
    )
    pressure = (GAMMA - 1.0) * (conserved[4] - kinetic)
    carried = momentum[axis_dir] / density
    columns = [
        momentum[axis_dir],
        momentum[0] * carried,
        momentum[1] * carried,
        momentum[2] * carried,
        (conserved[4] + pressure) * carried,
    ]
    columns[1 + axis_dir] = columns[1 + axis_dir] + pressure
    return jnp.stack(columns)


def volume_flux(conserved):
    return (axis_flux(0, conserved), axis_flux(1, conserved), axis_flux(2, conserved))


def face_trace(field_five, face):
    edge_index = 0 if face % 2 == 0 else 4
    return lax.index_in_dim(field_five, edge_index, 1 + face // 2, keepdims=False)


def add_to_face(field_five, face, face_term):
    edge_index = 0 if face % 2 == 0 else 4
    axis_dir = face // 2
    if axis_dir == 0:
        return field_five.at[:, edge_index].add(face_term)
    if axis_dir == 1:
        return field_five.at[:, :, edge_index].add(face_term)
    return field_five.at[:, :, :, edge_index].add(face_term)


def transposed_residual(adjoint, conserved, metric, viscosity, penalty, neighbor_trace):
    elements = adjoint.shape[-1]
    field_five = adjoint.reshape(5, 5, 5, 5, elements)
    state_five = conserved.reshape(5, 5, 5, 5, elements)
    weighted = tuple((sweep(field_five, axis_dir, True) for axis_dir in range(3)))
    primal_out, pullback = jax.vjp(volume_flux, state_five)
    volume = pullback(weighted)[0]
    viscous = (
        sweep(weighted[0], 0, False) + sweep(weighted[1], 1, False) + sweep(weighted[2], 2, False)
    )
    accumulated = metric * volume + viscosity * viscous
    for face in range(6):
        own_trace = face_trace(field_five, face)
        neighbor_part = neighbor_trace[:, :, :, face]
        face_state = face_trace(state_five, face)
        flux_out, face_pull = jax.vjp(functools.partial(axis_flux, face // 2), face_state)
        jacobian_term = face_pull(own_trace + neighbor_part)[0]
        normal_sign = 1.0 if face % 2 == 1 else -1.0
        face_term = (
            penalty[face] * (own_trace - neighbor_part) + 0.5 * normal_sign * metric * jacobian_term
        )
        accumulated = add_to_face(accumulated, face, face_term)
    return accumulated.reshape(5, 125, elements)


def pick_from_traces(gathered, neighbor_face):
    picked = jnp.zeros(gathered.shape[1:], gathered.dtype)
    for face in range(6):
        picked = jnp.where(neighbor_face == face, gathered[face], picked)
    return picked


def all_face_traces(adjoint):
    elements = adjoint.shape[-1]
    field_five = adjoint.reshape(5, 5, 5, 5, elements)
    return jnp.stack([face_trace(field_five, face) for face in range(6)], axis=0)


def orient_trace(picked, orientation, valid):
    oriented = jnp.where(orientation == 1, jnp.swapaxes(picked, 1, 2), picked)
    oriented = jnp.where(orientation == 2, jnp.flip(picked, 1), oriented)
    oriented = jnp.where(orientation == 3, jnp.flip(picked, 2), oriented)
    return jnp.where(valid, oriented, jnp.zeros_like(oriented))


def wall_sensitivity(adjoint, elem_index, face_index, partial_values):
    wall_count = elem_index.shape[0]
    volumes = jnp.take(adjoint, elem_index, axis=2).reshape(5, 5, 5, 5, wall_count)
    picked = jnp.zeros((5, 5, 5, wall_count), adjoint.dtype)
    for face in range(6):
        picked = jnp.where(face_index == face, face_trace(volumes, face), picked)
    return jnp.sum(partial_values * picked.reshape(1, 125, wall_count), axis=1)


def on_device(
    adjoint_start,
    objective_grad,
    conserved,
    metric_scale,
    time_step,
    viscosity,
    face_penalty,
    face_neighbor,
    neighbor_face,
    face_orient,
    wall_elem,
    wall_face,
    wall_partial,
    owner_device,
    owner_slot,
):
    elements = adjoint_start.shape[-1]
    span_size = lax.axis_size("span")
    chord_size = lax.axis_size("chord")
    wall_size = lax.axis_size("wall")
    partition_count = span_size * chord_size * wall_size
    span_stride = chord_size * wall_size
    own_part = (
        lax.axis_index("span") * chord_size + lax.axis_index("chord")
    ) * wall_size + lax.axis_index("wall")
    valid = face_neighbor >= 0
    safe_ids = jnp.maximum(face_neighbor, 0)
    offset = safe_ids // elements - own_part
    slot_number = jnp.where(
        offset == -span_stride,
        1,
        jnp.where(
            offset == span_stride,
            2,
            jnp.where(
                offset == -wall_size,
                3,
                jnp.where(
                    offset == wall_size, 4, jnp.where(offset == -1, 5, jnp.where(offset == 1, 6, 0))
                ),
            ),
        ),
    )
    slot_number = jnp.where(valid, slot_number, 0)
    local_elem = safe_ids % elements
    adjoint = adjoint_start
    flat_index = slot_number * elements + local_elem
    payload = all_face_traces(adjoint)
    pieces = [payload]
    for shift_by in (span_stride, -span_stride, wall_size, -wall_size, 1, -1):
        pieces.append(passed_along(payload, ("span", "chord", "wall"), shift_by))
    stacked = jnp.concatenate(pieces, axis=-1)
    gathered = jnp.take(stacked, flat_index, axis=stacked.ndim - 1)
    picked = pick_from_traces(gathered, neighbor_face)
    neighbor_trace = orient_trace(picked, face_orient, valid)
    residual = transposed_residual(
        adjoint, conserved, metric_scale, viscosity, face_penalty, neighbor_trace
    )
    adjoint = adjoint - time_step * (residual - objective_grad)
    values = wall_sensitivity(adjoint, wall_elem, wall_face, wall_partial)
    destination = owner_device[:, 0]
    design_ids = destination * DES_DEV + owner_slot
    dense_sens = jax.ops.segment_sum(values.T, design_ids, num_segments=partition_count * DES_DEV).T
    design_sens = lax.psum_scatter(
        dense_sens, ("span", "chord", "wall"), scatter_dimension=1, tiled=True
    )
    return (adjoint, design_sens)


def solution(mesh):
    in_specs = (
        P(None, None, ("span", "chord", "wall")),
        P(None, None, ("span", "chord", "wall")),
        P(None, None, ("span", "chord", "wall")),
        P(("span", "chord", "wall")),
        P(("span", "chord", "wall")),
        P(("span", "chord", "wall")),
        P(None, ("span", "chord", "wall")),
        P(None, ("span", "chord", "wall")),
        P(None, ("span", "chord", "wall")),
        P(None, ("span", "chord", "wall")),
        P(("span", "chord", "wall")),
        P(("span", "chord", "wall")),
        P(None, None, ("span", "chord", "wall")),
        P(("span", "chord", "wall"), None),
        P(("span", "chord", "wall")),
    )
    out_specs = (P(None, None, ("span", "chord", "wall")), P(None, ("span", "chord", "wall")))
    return jax.shard_map(
        on_device, mesh=mesh, in_specs=in_specs, out_specs=out_specs, check_vma=False
    )
```

profile of v0, /device:TPU:1, one launch (start us, length us, event | category | flops | bytes accessed | tf_op | source)
XLA Modules:
  0.0 1521.7 jit_solution(16551416724570016104)
XLA Ops:
  7.2 1.1 reshape.1366
  8.5 0.7 bitcast_dynamic-update-slice_fusion.1
  9.1 0.7 bitcast_dynamic-update-slice_fusion.4
  9.8 0.7 bitcast_dynamic-update-slice_fusion.2
  10.5 0.7 bitcast_dynamic-update-slice_fusion
  11.2 0.7 fusion.23
  11.8 0.7 fusion.25
  12.5 1.0 copy.390
  13.5 4.7 collective-permute-start
  18.2 1.3 collective-permute-start.1
  19.5 4.4 collective-permute-start.2
  23.8 1.3 collective-permute-start.3
  25.1 5.4 collective-permute-start.4
  30.7 0.6 fusion.20
  31.3 0.6 fusion.18
  31.9 0.6 convolution_bitcast_fusion.1
  32.6 1.4 fusion.14
  34.1 1.4 fusion.16
  35.5 0.7 fusion.146
  36.2 0.6 slice_bitcast_fusion.45
  36.8 0.6 broadcast_multiply_fusion
  37.6 0.6 broadcast_compare_fusion.15
  38.2 0.5 bitcast_add_fusion.5
  38.7 0.6 compare_and_fusion
  40.0 1.7 fusion.4
  41.9 1.0 copy.444
  43.0 1.3 collective-permute-done
  44.3 3.6 collective-permute-start.5
  47.9 2.1 copy_dynamic-update-slice_fusion.5
  50.0 2.1 copy_dynamic-update-slice_fusion.4
  52.1 2.0 copy_dynamic-update-slice_fusion.3
  54.1 2.1 copy_dynamic-update-slice_fusion.2
  56.2 2.1 copy_dynamic-update-slice_fusion.1
  58.2 1.0 copy_dynamic-update-slice_fusion
  59.2 42.3 %copy.402 = f32[6,5,5,5,896]{3,0,4,2,1:T(8,128)} copy(f32[6,5,5,5,896]{4,3,2,1,0:T(8,128)} %copy_dynamic-update-slice_fusion) | data formatting | bytes 5376000 | tf_op jit(solution)/shard_map/concatenate | solution.py:195
  101.5 55.1 %gather_fusion = f32[768,6,5,5,5]{4,1,3,2,0:T(8,128)} fusion(f32[6,5,5,5,896]{3,0,4,2,1:T(8,128)} %copy.402, s32[1024]{0:T(1024)S(1)} %pad_clamp_fusion.1), kind=kCustom, calls=%fused_computation | custom fusion | bytes 4611072 | tf_op jit(solution)/shard_map/jit(_take)/gather | solution.py:196
  156.6 40.0 %copy.404 = f32[6,128,6,5,5,5]{1,5,4,3,0,2:T(8,128)} copy(f32[6,128,6,5,5,5]{5,2,4,3,1,0:T(8,128)} %bitcast.23) | data formatting | bytes 4608000 | tf_op jit(solution)/shard_map/jit(_take)/gather | solution.py:196
  196.5 2.4 select_bitcast_fusion
  199.7 1.0 fusion.13
  200.7 0.8 add_add_fusion.11
  201.5 0.8 bitcast_add_fusion.1
  203.2 3.3 scatter-add.34
  206.6 3.3 scatter-add.42
  210.6 0.8 gather_fusion.1
  212.4 8.0 scatter_custom_fusion
  220.4 0.9 copy.448
  221.3 1292.1 %reduce-scatter.2.cloned.1.call-done = f32[3,128]{0,1:T(8,128)} async-done(((f32[3,32768]{0,1:T(8,128)}), f32[3,128]{0,1:T(8,128)}) %reduce-scatter.2.cloned.1.call-update) | async-done | bytes 1552 | tf_op jit(solution)/shard_map/reduce_scatter | solution.py:207
  1513.4 1.5 copy.449
  (139 shorter events, 4.7 us)
Async XLA Ops:
  7.2 23.5 %copy-start.8 = (f32[5,5,1,1,1]{0,1,4,3,2:T(8,128)S(1)}, f32[5,5,1,1,1]{0,1,4,3,2:T(8,128)}, u32[]{:S(2)}) copy-start(f32[5,5,1,1,1]{0,1,4,3,2:T(8,128)} %constant.404) | copy-start | bytes 304
  7.2 23.3 %copy-start.2 = (f32[5,125,128]{2,1,0:T(8,128)S(1)}, f32[5,125,128]{2,1,0:T(8,128)}, u32[]{:S(2)}) copy-start(f32[5,125,128]{2,1,0:T(8,128)} %param.35) | copy-start | bytes 960004
  7.2 1506.2 %reduce-scatter.2.cloned.1.call-start = ((), (), s32[]{:S(2)}) async-start(), calls=%async_computation.1 | async-start | bytes 16842752 | tf_op jit(solution)/shard_map/reduce_scatter | solution.py:207
  13.5 30.9 %collective-permute-start = (f32[6,5,5,5,128]{4,0,3,2,1:T(8,128)}, f32[6,5,5,5,128]{4,0,3,2,1:T(8,128)}, u32[]{:S(2)}, u32[]{:S(2)}) collective-permute-start(f32[6,5,5,5,128]{4,0,3,2,1:T(8,128)} %copy.390), channel_id=1, source_target_pairs={{0,16},{1,17},{2,18},{3,19},{4,20},{5,21},{6,22},{7,23},{8,24},{9,... | collective-permute-start | bytes 1152008 | tf_op jit(solution)/shard_map/ppermute | solution.py:19
  18.2 31.8 %collective-permute-start.1 = (f32[6,5,5,5,128]{4,0,3,2,1:T(8,128)}, f32[6,5,5,5,128]{4,0,3,2,1:T(8,128)}, u32[]{:S(2)}, u32[]{:S(2)}) collective-permute-start(f32[6,5,5,5,128]{4,0,3,2,1:T(8,128)} %copy.390), channel_id=1, source_target_pairs={{16,0},{17,1},{18,2},{19,3},{20,4},{21,5},{22,6},{23,7},{24,8},{25... | collective-permute-start | bytes 1152008 | tf_op jit(solution)/shard_map/ppermute | solution.py:19
  19.5 32.6 %collective-permute-start.2 = (f32[6,5,5,5,128]{4,0,3,2,1:T(8,128)}, f32[6,5,5,5,128]{4,0,3,2,1:T(8,128)}, u32[]{:S(2)}, u32[]{:S(2)}) collective-permute-start(f32[6,5,5,5,128]{4,0,3,2,1:T(8,128)} %copy.390), channel_id=1, source_target_pairs={{0,2},{1,3},{2,4},{3,5},{4,6},{5,7},{6,8},{7,9},{8,10},{9,11},{10,... | collective-permute-start | bytes 1152008 | tf_op jit(solution)/shard_map/ppermute | solution.py:19
  23.8 30.2 %collective-permute-start.3 = (f32[6,5,5,5,128]{4,0,3,2,1:T(8,128)}, f32[6,5,5,5,128]{4,0,3,2,1:T(8,128)}, u32[]{:S(2)}, u32[]{:S(2)}) collective-permute-start(f32[6,5,5,5,128]{4,0,3,2,1:T(8,128)} %copy.390), channel_id=1, source_target_pairs={{2,0},{3,1},{4,2},{5,3},{6,4},{7,5},{8,6},{9,7},{10,8},{11,9},{12,... | collective-permute-start | bytes 1152008 | tf_op jit(solution)/shard_map/ppermute | solution.py:19
  25.1 31.0 %collective-permute-start.4 = (f32[6,5,5,5,128]{4,0,3,2,1:T(8,128)}, f32[6,5,5,5,128]{4,0,3,2,1:T(8,128)}, u32[]{:S(2)}, u32[]{:S(2)}) collective-permute-start(f32[6,5,5,5,128]{4,0,3,2,1:T(8,128)} %copy.390), channel_id=1, source_target_pairs={{0,1},{1,2},{2,3},{3,4},{4,5},{5,6},{6,7},{7,8},{8,9},{9,10},{10,1... | collective-permute-start | bytes 1152008 | tf_op jit(solution)/shard_map/ppermute | solution.py:19
  30.5 5.0 copy-start.12
  30.5 5.7 copy-start.15
  30.6 6.3 copy-start.34
  30.7 6.9 copy-start.29
  30.7 6.9 copy-start.30
  30.7 7.5 copy-start.31
  30.7 7.5 copy-start.32
  30.7 8.0 copy-start.13
  30.7 8.0 copy-start.14
  37.4 2.5 copy-start.33
  37.6 2.4 copy-start.4
  37.6 2.4 copy-start.5
  39.6 2.1 copy-start.3
  39.8 2.2 copy-start.6
  44.3 13.9 collective-permute-start.5
  199.2 3.4 copy-start
  199.6 3.0 copy-start.10
  199.7 3.0 copy-start.27
  199.7 3.0 copy-start.11
  199.7 3.0 copy-start.26
  199.7 3.1 copy-start.25
  199.7 3.1 copy-start.24
  199.7 3.3 copy-start.9
  200.7 2.4 copy-start.23
  202.3 8.0 copy-start.1
  202.3 8.0 copy-start.28
  202.8 8.8 copy-start.16
  209.9 2.2 copy-start.17
  209.9 2.2 copy-start.18
  209.9 2.2 copy-start.19
  209.9 2.2 copy-start.20
  210.0 2.2 copy-start.21
  210.0 2.2 copy-start.22
  210.0 2.3 copy-start.7
Sparse Core Ops, SparseCore 0:
  220.5 1292.8 reduce-scatter.1
where the time goes:
time: 1530 us; the launch traced here: 1520 us
  waiting for transfers between devices  1290 us (84%)
  local copies, waits for them, and re-layouts  169 us (11%)
  starting transfers between devices  20.7 us (1%)
  other arithmetic  17.3 us (1%)
    reduce_scatter x1, waiting for transfers between devices, on_device(): lax.psum_scatter(dense_sens, ('span', 'chord', 'wall'), scatter_dimension...  1290 us
    gather x2, local copies, waits for them, and re-layouts, on_device(): gathered = jnp.take(stacked, flat_index, axis=stacked.ndim - 1)  95 us
    concatenate x2, local copies, waits for them, and re-layouts, on_device(): stacked = jnp.concatenate(pieces, axis=-1)  43.3 us
  transfers between devices with their start and end apart: 7, of which 2 were waited for; matrix products, arithmetic and copies ran while one was open for 2% of the time, Pallas kernels for 0%

commit v1 on v0

v1 whole, which is shorter than its diff:
```python
import functools
import math

import jax
import jax.numpy as jnp
import numpy as np
from jax import lax
from jax.experimental import pallas as pl
from jax.experimental.pallas import tpu as pltpu
from jax.sharding import PartitionSpec as P

AXES = ("span", "chord", "wall")
MESH = pl.DeviceIdType.MESH
F32 = jnp.float32
BF16 = jnp.bfloat16
I32 = jnp.int32
E = 128
REQ = 64
HALO = 5
OPPOSITE = (1, 0, 3, 2, 4)
G = 0.4


def derivative_table():
    points = [-1.0, -math.sqrt(3.0 / 7.0), 0.0, math.sqrt(3.0 / 7.0), 1.0]
    barycentric = []
    for i in range(5):
        product_value = 1.0
        for j in range(5):
            if j != i:
                product_value = product_value * (points[i] - points[j])
        barycentric.append(1.0 / product_value)
    matrix_values = np.zeros((5, 5))
    for i in range(5):
        for j in range(5):
            if j != i:
                matrix_values[i, j] = barycentric[j] / barycentric[i] / (points[i] - points[j])
        matrix_values[i, i] = -np.sum(matrix_values[i])
    return matrix_values


def face_node(face, a, b):
    edge = 0 if face % 2 == 0 else 4
    index = {0: (edge, a, b), 1: (a, edge, b), 2: (a, b, edge)}[face // 2]
    return 25 * index[0] + 5 * index[1] + index[2]


def oriented(orient, a, b):
    return {0: (a, b), 1: (b, a), 2: (4 - a, b), 3: (a, 4 - b)}[orient]


def split_table(table):
    high = table.astype(np.float32).astype(jnp.bfloat16)
    low = (table - high.astype(np.float64)).astype(np.float32).astype(jnp.bfloat16)
    return high, low


@functools.cache
def tables():
    d = derivative_table()
    eye = np.eye(5)
    ends = np.zeros((5, 5))
    ends[0, 0], ends[4, 4] = -0.5, 0.5
    along = [
        lambda m: np.kron(m, np.kron(eye, eye)),
        lambda m: np.kron(eye, np.kron(m, eye)),
        lambda m: np.kron(eye, np.kron(eye, m)),
    ]
    sweeps = np.zeros((512, 128))
    for axis in range(3):
        sweeps[128 * axis : 128 * axis + 125, :125] = along[axis](d.T + ends)
        sweeps[384:509, :125] += along[axis](d) @ along[axis](d.T)
    sweep_high, sweep_low = split_table(sweeps)
    traces = np.zeros((192, 128))
    to_nodes = np.zeros((3, 128, 256))
    penalties = np.zeros((512, 32))
    for face in range(6):
        axis, sign = face // 2, (1.0 if face % 2 else -1.0)
        for a in range(5):
            for b in range(5):
                node = face_node(face, a, b)
                traces[32 * face + 5 * a + b, node] = 1.0
                for term in range(3):
                    penalties[128 * axis + node, 8 * term + face] = 2.0 * sign
                    penalties[384 + node, 8 * term + face] = 1.0
                for orient in range(4):
                    oa, ob = oriented(orient, a, b)
                    column = ((face % 2) * 4 + orient) * 32 + 5 * oa + ob
                    to_nodes[axis, node, column] = 0.5 * sign
    dense = np.zeros((128, 160))
    for field in range(5):
        for ab in range(25):
            dense[25 * field + ab, 32 * field + ab] = 1.0
    as_bf16 = lambda t: t.astype(np.float32).astype(jnp.bfloat16)
    return (
        np.concatenate([sweep_high, sweep_low], 0),
        as_bf16(traces),
        as_bf16(to_nodes),
        as_bf16(penalties),
        as_bf16(dense),
        as_bf16(dense.T.copy()),
    )


def split(x):
    high = x.astype(BF16)
    return high, (x - high.astype(F32)).astype(BF16)


def mm(a, b):
    return lax.dot_general(a, b, (((1,), (0,)), ((), ())), preferred_element_type=F32)


def mm_nt(a, b):
    return lax.dot_general(a, b, (((1,), (1,)), ((), ())), preferred_element_type=F32)


def iota(shape, dim):
    return lax.broadcasted_iota(I32, shape, dim)


def one_if(condition):
    return jnp.where(condition, 1.0, 0.0)


def kernel(
    sizes,
    psi_hbm,
    obj_hbm,
    u_hbm,
    wp_hbm,
    metric_hbm,
    dt_hbm,
    visc_hbm,
    pen_hbm,
    fn_hbm,
    nf_hbm,
    fo_hbm,
    we_hbm,
    wf_hbm,
    od_hbm,
    os_hbm,
    sweeps_hbm,
    traces_hbm,
    to_nodes_hbm,
    penalties_hbm,
    dense_hbm,
    dense_t_hbm,
    adj_hbm,
    sens_ref,
    metric_ref,
    dt_ref,
    visc_ref,
    pen_ref,
    fn_ref,
    nf_ref,
    fo_ref,
    we_ref,
    wf_ref,
    od_ref,
    os_ref,
    sweeps_ref,
    traces_ref,
    to_nodes_ref,
    penalties_ref,
    dense_ref,
    dense_t_ref,
    psi,
    obj,
    u,
    wp,
    wpad,
    adj,
    psib,
    xp,
    xd,
    local_hot,
    request_hot,
    req_out,
    req_in,
    resp_out,
    resp_in,
    swept,
    pen_nodes,
    rhs,
    jump,
    wall_hot,
    owner_hot,
    send_a,
    recv_a,
    send_b,
    recv_b,
    in_sem,
    out_sem,
    req_send_sem,
    req_recv_sem,
    resp_send_sem,
    resp_recv_sem,
    a_send_sem,
    a_recv_sem,
    b_send_sem,
    b_recv_sem,
):
    n_span, n_chord, n_wall = sizes
    n_plane = n_chord * n_wall
    s, c, w = (lax.axis_index(name) for name in AXES)
    part = (s * n_chord + c) * n_wall + w
    plane = c * n_wall + w

    sources = {
        "fn": (fn_hbm, fn_ref),
        "nf": (nf_hbm, nf_ref),
        "psi": (psi_hbm, psi),
        "traces": (traces_hbm, traces_ref),
        "dense": (dense_hbm, dense_ref),
        "sweeps": (sweeps_hbm, sweeps_ref),
        "pen": (pen_hbm, pen_ref),
        "penalties": (penalties_hbm, penalties_ref),
        "we": (we_hbm, we_ref),
        "wf": (wf_hbm, wf_ref),
        "wp": (wp_hbm, wp),
        "od": (od_hbm, od_ref),
        "os": (os_hbm, os_ref),
        "fo": (fo_hbm, fo_ref),
        "dense_t": (dense_t_hbm, dense_t_ref),
        "to_nodes": (to_nodes_hbm, to_nodes_ref),
        "u": (u_hbm, u),
        "obj": (obj_hbm, obj),
        "metric": (metric_hbm, metric_ref),
        "dt": (dt_hbm, dt_ref),
        "visc": (visc_hbm, visc_ref),
    }
    loads = {}
    for i, (name, (src, dst)) in enumerate(sources.items()):
        loads[name] = pltpu.make_async_copy(src, dst, in_sem.at[i])
        loads[name].start()

    def ready(*names):
        for name in names:
            loads[name].wait()

    barrier = pltpu.get_barrier_semaphore()
    for k in range(1, n_span):
        pl.semaphore_signal(
            barrier, inc=1, device_id=(lax.rem(s + k, n_span), c, w), device_id_type=MESH
        )
    for k in range(1, n_plane):
        there = lax.rem(plane + k, n_plane)
        pl.semaphore_signal(
            barrier,
            inc=1,
            device_id=(s, there // n_wall, lax.rem(there, n_wall)),
            device_id_type=MESH,
        )

    ready("fn", "nf")
    fn, nf = fn_ref[...], nf_ref[...]
    offset = jnp.where(fn >= 0, lax.shift_right_arithmetic(fn, 7) - part, 1 << 20)
    elem = jnp.bitwise_and(fn, E - 1)
    slot = iota((8, E), 0)
    wanted = jnp.where(slot == 4, 1 - 2 * w, 1 << 21)
    for j, step in enumerate((-n_plane, n_plane, -n_wall, n_wall)):
        wanted = jnp.where(slot == j, step, wanted)
    named = [offset[f : f + 1] == wanted for f in range(6)]
    before = jnp.concatenate(
        [one_if(iota((E, E), 0) < iota((E, E), 1)), jnp.ones((E, E), F32)], 1
    ).astype(BF16)
    counts = mm(jnp.concatenate([one_if(m) for m in named], 0).astype(BF16), before)
    base = jnp.zeros((8, E), F32)
    place = iota((REQ, E), 0).astype(F32)
    sub16 = iota((16, E), 0)
    codes = []
    for f in range(6):
        rank = jnp.where(named[f], counts[8 * f : 8 * f + 8, :E] + base, -1.0)
        base = base + counts[8 * f : 8 * f + 8, E:]
        for j in range(HALO):
            request_hot[REQ * j : REQ * (j + 1), E * f : E * (f + 1)] = one_if(
                rank[j : j + 1] == place
            ).astype(BF16)
        code = jnp.where(
            sub16 == 0, elem[f : f + 1], jnp.where(sub16 == 1, nf[f : f + 1], (sub16 == 2).astype(I32))
        )
        codes.append(code.astype(F32).astype(BF16))
    codes = jnp.concatenate(codes, 1)
    for j in range(HALO):
        got = mm_nt(codes, request_hot[REQ * j : REQ * (j + 1), :])
        req_out[j] = jnp.zeros((1, E), F32)
        req_out[j, :, 0:REQ] = got[0:1] + 128.0 * got[1:2] + 2048.0 * (1.0 - got[2:3])

    pl.semaphore_wait(barrier, n_span - 1 + n_plane - 1)
    beside = (
        (lax.rem(s + n_span - 1, n_span), c, w),
        (lax.rem(s + 1, n_span), c, w),
        (s, lax.rem(c + n_chord - 1, n_chord), w),
        (s, lax.rem(c + 1, n_chord), w),
        (s, c, 1 - w),
    )
    requests = [
        pltpu.make_async_remote_copy(
            src_ref=req_out.at[j],
            dst_ref=req_in.at[OPPOSITE[j]],
            send_sem=req_send_sem.at[j],
            recv_sem=req_recv_sem.at[OPPOSITE[j]],
            device_id=beside[j],
            device_id_type=MESH,
        )
        for j in range(HALO)
    ]
    for copy in requests:
        copy.start()

    ready("psi", "traces", "dense")
    for field in range(5):
        psib[0, 112:128, E * field : E * (field + 1)] = jnp.zeros((16, E), BF16)
        psib[1, 112:128, E * field : E * (field + 1)] = jnp.zeros((16, E), BF16)
        high, low = split(psi[field])
        psib[0, 0:125, E * field : E * (field + 1)] = high
        psib[1, 0:125, E * field : E * (field + 1)] = low
    for half in range(2):
        got = mm(traces_ref[...], psib[half]).astype(BF16)
        for field in range(5):
            for f in range(6):
                xp[160 * half + 32 * field : 160 * half + 32 * (field + 1), E * f : E * (f + 1)] = got[
                    32 * f : 32 * (f + 1), E * field : E * (field + 1)
                ]
        xd[128 * half : 128 * (half + 1), :] = mm(
            dense_ref[...], xp[160 * half : 160 * (half + 1), :]
        ).astype(BF16)

    for copy in requests:
        copy.wait_recv()
    asked = jnp.zeros((E, E), F32)
    rows = iota((E, E), 0)
    for j in range(HALO):
        asked = jnp.where(rows == j, req_in[j], asked)
    asked = asked.T
    columns = iota((REQ, 6 * E), 1).astype(F32)
    responses = []
    for j in range(HALO):
        hot = one_if(asked[0:REQ, j : j + 1] == columns).astype(BF16)
        got = mm_nt(hot, xd[...])
        resp_out[j] = got[:, :E] + got[:, E:]
        copy = pltpu.make_async_remote_copy(
            src_ref=resp_out.at[j],
            dst_ref=resp_in.at[OPPOSITE[j]],
            send_sem=resp_send_sem.at[j],
            recv_sem=resp_recv_sem.at[OPPOSITE[j]],
            device_id=beside[j],
            device_id_type=MESH,
        )
        copy.start()
        responses.append(copy)

    for f in range(6):
        code = jnp.where(offset[f : f + 1] == 0, elem[f : f + 1] + E * nf[f : f + 1], -1)
        for g in range(6):
            local_hot[E * g : E * (g + 1), E * f : E * (f + 1)] = one_if(
                code == iota((E, E), 0) + E * g
            ).astype(BF16)
    near = mm(xp[...], local_hot[...])
    ready("sweeps", "pen", "penalties")
    swept[...] = (
        mm(sweeps_ref[0:512], psib[0]) + mm(sweeps_ref[512:1024], psib[0]) + mm(sweeps_ref[0:512], psib[1])
    )
    pen8 = jnp.concatenate([pen_ref[...], jnp.zeros((2, E), F32)], 0)
    pen_high, pen_rest = pen8.astype(BF16), pen8
    pen_terms = []
    for _ in range(3):
        pen_high = pen_rest.astype(BF16).astype(F32)
        pen_terms.append(pen_high)
        pen_rest = pen_rest - pen_high
    pen_terms.append(jnp.zeros((8, E), F32))
    pen_nodes[...] = mm(penalties_ref[...], jnp.concatenate(pen_terms, 0).astype(BF16))

    ready("we", "wf", "wp", "od", "os", "fo", "dense_t", "to_nodes")
    fo = fo_ref[...]
    wall_code = we_ref[...] + E * wf_ref[...]
    for g in range(6):
        wall_hot[E * g : E * (g + 1), :] = one_if(wall_code == iota((E, E), 0) + E * g).astype(BF16)
    for x in range(3):
        for field in range(5):
            wpad[x, field] = jnp.zeros((32, E), F32)
            wpad[x, field, 0:25] = wp[x, 25 * field : 25 * (field + 1)]
    owner = od_ref[...]
    owner_rows = jnp.broadcast_to(owner.astype(F32), (E, E))
    owner_columns = owner_rows.T
    earlier = one_if((owner_rows == owner_columns) & (iota((E, E), 1) < iota((E, E), 0)))
    rank = jnp.sum(earlier, axis=1, keepdims=True)
    owner_span = lax.shift_right_arithmetic(owner, n_plane.bit_length() - 1)
    owner_plane = jnp.bitwise_and(owner_columns.astype(I32), n_plane - 1).astype(F32)
    lane = iota((E, E), 1).astype(F32)
    for v in range(4):
        owner_hot[E * v : E * (v + 1), :] = one_if(lane == 8.0 * owner_plane + rank + 2.0 * v).astype(BF16)
    to_span = one_if(iota((16, E), 0) == owner_span)

    for copy in responses:
        copy.wait_recv()
    answered = jnp.concatenate([resp_in[j] for j in range(HALO)], 0)
    answered_high, answered_low = split(answered)
    far = mm(
        jnp.concatenate(
            [mm_nt(dense_t_ref[...], answered_high), mm_nt(dense_t_ref[...], answered_low)], 0
        ).astype(BF16),
        request_hot[...],
    )
    found = near + far
    trace_high, trace_low = split(found[:160] + found[160:])
    for f in range(6):
        for o in range(4):
            mask = one_if(jnp.broadcast_to(fo[f : f + 1] == o, (32, E))).astype(BF16)
            row = ((f % 2) * 4 + o) * 32
            for field in range(5):
                for half, trace in enumerate((trace_high, trace_low)):
                    rhs[f // 2, 256 * half + row : 256 * half + row + 32, E * field : E * (field + 1)] = (
                        trace[32 * field : 32 * (field + 1), E * f : E * (f + 1)] * mask
                    )
    for axis in range(3):
        table = jnp.concatenate([to_nodes_ref[axis], to_nodes_ref[axis]], 1)
        jump[axis] = mm(table, rhs[axis])

    ready("u", "obj", "metric", "dt", "visc")
    metric, dt, visc = metric_ref[...], dt_ref[...], visc_ref[...]
    for field in range(5):
        adj[field, 120:128] = jnp.zeros((8, E), F32)
    for start in range(0, 125, 8):
        stop = min(start + 8, 125)
        cut = slice(start, stop)

        def lanes(field):
            return slice(E * field, E * (field + 1))

        rho, m1, m2, m3, energy = (u[field, cut] for field in range(5))
        inverse = 1.0 / rho
        vel = (m1 * inverse, m2 * inverse, m3 * inverse)
        kinetic = 0.5 * (vel[0] * vel[0] + vel[1] * vel[1] + vel[2] * vel[2])
        pressure = G * (energy - rho * kinetic)
        enthalpy = (energy + pressure) * inverse
        out = [0.0] * 5
        a_sum = 0.0
        diffused = []
        for axis in range(3):
            jumps = [jump[axis, cut, lanes(field)] for field in range(5)]
            wd = [
                swept[128 * axis + start : 128 * axis + stop, lanes(field)] + jumps[field]
                for field in range(5)
            ]
            pen = pen_nodes[128 * axis + start : 128 * axis + stop]
            diffused.append([pen * jumps[field] for field in range(5)])
            vd = vel[axis]
            carried = wd[1] * vel[0] + wd[2] * vel[1] + wd[3] * vel[2] + enthalpy * wd[4]
            a = wd[1 + axis] + vd * wd[4]
            a_sum = a_sum + a
            out[0] = out[0] - vd * carried
            for i in range(3):
                out[1 + i] = out[1 + i] + vd * wd[1 + i]
            out[1 + axis] = out[1 + axis] + (wd[0] + carried)
            out[4] = out[4] + vd * wd[4]
        ga = G * a_sum
        out[0] = out[0] + kinetic * ga
        for i in range(3):
            out[1 + i] = out[1 + i] - vel[i] * ga
        out[4] = out[4] + ga
        pen = pen_nodes[384 + start : 384 + stop]
        for field in range(5):
            old = psi[field, cut]
            residual = (
                metric * out[field]
                + visc * swept[384 + start : 384 + stop, lanes(field)]
                + (pen * old - (diffused[0][field] + diffused[1][field] + diffused[2][field]))
            )
            adj[field, cut] = old - dt * (residual - obj[field, cut])
    store = pltpu.make_async_copy(adj.at[:, 0:125], adj_hbm, out_sem)
    store.start()

    for field in range(5):
        high, low = split(adj[field])
        psib[0, :, E * field : E * (field + 1)] = high
        psib[1, :, E * field : E * (field + 1)] = low
    for half in range(2):
        got = mm(traces_ref[...], psib[half]).astype(BF16)
        for field in range(5):
            for f in range(6):
                xp[160 * half + 32 * field : 160 * half + 32 * (field + 1), E * f : E * (f + 1)] = got[
                    32 * f : 32 * (f + 1), E * field : E * (field + 1)
                ]
    taken = mm(xp[...], wall_hot[...])
    taken = taken[:160] + taken[160:]
    values = [os_ref[...].astype(F32)]
    for x in range(3):
        total = wpad[x, 0] * taken[0:32]
        for field in range(1, 5):
            total = total + wpad[x, field] * taken[32 * field : 32 * (field + 1)]
        values.append(jnp.sum(total, axis=0, keepdims=True))
    spread = jnp.concatenate([to_span * value for value in values], 1)
    terms = []
    for _ in range(3):
        term = spread.astype(BF16)
        terms.append(term)
        spread = spread - term.astype(F32)
    sent = mm(jnp.concatenate(terms, 0), owner_hot[...])
    sent = sent[0:16] + sent[16:32] + sent[32:48]

    for k in range(n_span):
        send_a[k] = sent[k : k + 1]
    copies = []
    for k in range(1, n_span):
        there = lax.rem(s + k, n_span)
        copy = pltpu.make_async_remote_copy(
            src_ref=send_a.at[there],
            dst_ref=recv_a.at[s],
            send_sem=a_send_sem.at[k],
            recv_sem=a_recv_sem.at[k],
            device_id=(there, c, w),
            device_id_type=MESH,
        )
        copy.start()
        copies.append(copy)
    recv_a[s] = send_a[s]
    for copy in copies:
        copy.wait_recv()
    arrived = jnp.zeros((E, E), F32)
    for k in range(n_span):
        arrived = jnp.where(rows == k, recv_a[k], arrived)
    arrived = arrived.T
    for k in range(n_plane):
        send_b[k] = arrived[8 * k : 8 * (k + 1)]
    copies_b = []
    for k in range(1, n_plane):
        there = lax.rem(plane + k, n_plane)
        copy = pltpu.make_async_remote_copy(
            src_ref=send_b.at[there],
            dst_ref=recv_b.at[plane],
            send_sem=b_send_sem.at[k],
            recv_sem=b_recv_sem.at[k],
            device_id=(s, there // n_wall, lax.rem(there, n_wall)),
            device_id_type=MESH,
        )
        copy.start()
        copies_b.append(copy)
    recv_b[plane] = send_b[plane]
    for copy in copies_b:
        copy.wait_recv()
    design = iota((8, E), 1).astype(F32)
    total = jnp.zeros((8, E), F32)
    for k in range(n_plane):
        block = recv_b[k]
        slots = jnp.concatenate([block[0:2]] * 4, 0)
        for j in range(n_span):
            total = total + jnp.where(slots[:, j : j + 1] == design, block[:, j : j + 1], 0.0)
    for x in range(3):
        sens_ref[x : x + 1] = total[2 + 2 * x : 3 + 2 * x] + total[3 + 2 * x : 4 + 2 * x]

    for copy in requests + responses + copies + copies_b:
        copy.wait_send()
    store.wait()


def on_device(sizes, *args):
    (psi, obj, u, metric, dt, visc, pen, fn, nf, fo, we, wf, wp, od, os_) = args
    row = lambda x: x.reshape(1, E)
    vmem = pl.BlockSpec(memory_space=pltpu.VMEM)
    hbm = pl.BlockSpec(memory_space=pltpu.HBM)
    n_span, n_chord, n_wall = sizes
    n_plane = n_chord * n_wall
    consts = tuple(jnp.asarray(t) for t in tables())
    return pl.pallas_call(
        functools.partial(kernel, sizes),
        out_shape=(
            jax.ShapeDtypeStruct((5, 125, E), F32),
            jax.ShapeDtypeStruct((3, E), F32),
        ),
        in_specs=[hbm] * (15 + len(consts)),
        out_specs=(hbm, vmem),
        scratch_shapes=[
            *[pltpu.VMEM((1, E), F32)] * 3,
            pltpu.VMEM((6, E), F32),
            *[pltpu.VMEM((6, E), I32)] * 3,
            *[pltpu.VMEM((1, E), I32)] * 4,
            *[pltpu.VMEM(t.shape, BF16) for t in consts],
            pltpu.VMEM((5, 125, E), F32),
            pltpu.VMEM((5, 125, E), F32),
            pltpu.VMEM((5, 125, E), F32),
            pltpu.VMEM((3, 125, E), F32),
            pltpu.VMEM((3, 5, 32, E), F32),
            pltpu.VMEM((5, 128, E), F32),
            pltpu.VMEM((2, 128, 5 * E), BF16),
            pltpu.VMEM((320, 6 * E), BF16),
            pltpu.VMEM((256, 6 * E), BF16),
            pltpu.VMEM((6 * E, 6 * E), BF16),
            pltpu.VMEM((HALO * REQ, 6 * E), BF16),
            pltpu.VMEM((HALO, 1, E), F32),
            pltpu.VMEM((HALO, 1, E), F32),
            pltpu.VMEM((HALO, REQ, E), F32),
            pltpu.VMEM((HALO, REQ, E), F32),
            pltpu.VMEM((512, 5 * E), F32),
            pltpu.VMEM((512, E), F32),
            pltpu.VMEM((3, 512, 5 * E), BF16),
            pltpu.VMEM((3, 128, 5 * E), F32),
            pltpu.VMEM((6 * E, E), BF16),
            pltpu.VMEM((4 * E, E), BF16),
            pltpu.VMEM((n_span, 1, E), F32),
            pltpu.VMEM((n_span, 1, E), F32),
            pltpu.VMEM((n_plane, 8, E), F32),
            pltpu.VMEM((n_plane, 8, E), F32),
            pltpu.SemaphoreType.DMA((15 + len(consts),)),
            pltpu.SemaphoreType.DMA,
            pltpu.SemaphoreType.DMA((HALO,)),
            pltpu.SemaphoreType.DMA((HALO,)),
            pltpu.SemaphoreType.DMA((HALO,)),
            pltpu.SemaphoreType.DMA((HALO,)),
            pltpu.SemaphoreType.DMA((n_span,)),
            pltpu.SemaphoreType.DMA((n_span,)),
            pltpu.SemaphoreType.DMA((n_plane,)),
            pltpu.SemaphoreType.DMA((n_plane,)),
        ],
        compiler_params=pltpu.CompilerParams(
            collective_id=0, has_side_effects=True, vmem_limit_bytes=60 * 2**20
        ),
        name="adjoint_step",
    )(
        psi,
        obj,
        u,
        wp,
        row(metric),
        row(dt),
        row(visc),
        pen,
        fn,
        nf,
        fo,
        row(we),
        row(wf),
        row(od),
        row(os_),
        *consts,
    )


def solution(mesh):
    whole = P(None, None, AXES)
    plane = P(None, AXES)
    line = P(AXES)
    in_specs = (
        (whole,) * 3 + (line,) * 3 + (plane,) * 4 + (line,) * 2 + (whole, P(AXES, None), line)
    )
    sizes = tuple(mesh.shape[name] for name in AXES)
    return jax.shard_map(
        functools.partial(on_device, sizes),
        mesh=mesh,
        in_specs=in_specs,
        out_specs=(whole, plane),
        check_vma=False,
    )
```

time: 1530 us -> 36.9 us (0.02)
  waiting for transfers between devices: 1290 us -> 0 us
  local copies, waits for them, and re-layouts: 169 us -> 2.3 us
  Pallas kernels: 0 us -> 33.9 us
  starting transfers between devices: 20.7 us -> 0 us
  other arithmetic: 17.3 us -> 0 us
    reduce_scatter x1 -> x0, waiting for transfers between devices: 1290 us -> none  [on_device(): lax.psum_scatter(dense_sens, ('span', 'chord', 'wall'), scatter_dimension...]
    gather x5 -> x0, local copies, waits for them, and re-layouts: 96.1 us -> none  [the longest x2 95 us: on_device(): gathered = jnp.take(stacked, flat_index, axis=stacked.ndim - 1)]
    concatenate x2 -> x0, local copies, waits for them, and re-layouts: 43.3 us -> none  [on_device(): stacked = jnp.concatenate(pieces, axis=-1)]
    pallas_call x0 -> x1, Pallas kernels: none -> 33.9 us  [on_device(): pl.pallas_call(functools.partial(kernel, sizes), out_shape=(jax.ShapeDtyp...]
    ppermute x6 -> x0, starting transfers between devices: 20.6 us -> none  [passed_along(): return lax.ppermute(block, axis, route)]
  transfers between devices with their start and end apart: 7 -> 0, of which waited for: 2 -> 0; matrix products, arithmetic and copies ran while one was open for 2% -> 0% of each run, Pallas kernels for 0% -> 0%
where the time goes in v1:
time: 36.9 us; the launch traced here: 36.8 us
  Pallas kernels  33.9 us (92%)
  local copies, waits for them, and re-layouts  2.3 us (6%)
  between operations  0.65 us (2%)
    pallas_call x1, Pallas kernels, on_device(): pl.pallas_call(functools.partial(kernel, sizes), out_shape=(jax.ShapeDtyp...  33.9 us
    unnamed x4, local copies, waits for them, and re-layouts  2.3 us

profile of v1, /device:TPU:1, one launch (start us, length us, event | category | flops | bytes accessed | tf_op | source)
XLA Modules:
  0.0 36.8 jit_solution(16359704524367266650)
XLA Ops:
  0.6 33.9 %adjoint_step.1 = (f32[5,125,128]{2,1,0:T(8,128)}, f32[3,128]{1,0:T(4,128)}) custom-call(f32[5,125,128]{2,1,0:T(8,128)} %psi_hbm.1, f32[5,125,128]{2,1,0:T(8,128)} %obj_hbm.1, f32[5,125,128]{2,1,0:T(8,128)} %u_hbm.1, f32[3,125,128]{2,1,0:T(8,128)} %wp_hbm.1, f32[1,128]{1,0:T(1,128)} %bitcast.7, f32[1,128]{1,0:T(1,128)} %bitcast.8, f32[1,128]{1,0:T(1,128)} %bitcast.9, ...), custom_call_target="tpu_custom_call" | custom-call | tf_op jit(solution)/shard_map/adjoint_step/pallas_call | solution.py:566
  34.5 0.0 copy-start
  34.5 1.7 %copy.25 = f32[5,125,128]{2,1,0:T(8,128)} copy(f32[5,125,128]{2,1,0:T(8,128)} %get-tuple-element.4) | data formatting | bytes 640000
  36.2 0.0 copy-done
  36.2 0.6 %copy.26 = f32[3,128]{1,0:T(4,128)} copy(f32[3,128]{1,0:T(4,128)S(1)} %copy-done) | data formatting | bytes 3072
Async XLA Ops:
  34.5 1.7 %copy-start = (f32[3,128]{1,0:T(4,128)S(1)}, f32[3,128]{1,0:T(4,128)}, u32[]{:S(2)}) copy-start(f32[3,128]{1,0:T(4,128)} %get-tuple-element.5) | copy-start | bytes 4612

commit v2 on v1

v2 whole, which is shorter than its diff:
```python
import functools
import math

import jax
import jax.numpy as jnp
import numpy as np
from jax import lax
from jax.experimental import pallas as pl
from jax.experimental.pallas import tpu as pltpu
from jax.sharding import PartitionSpec as P

AXES = ("span", "chord", "wall")
MESH = pl.DeviceIdType.MESH
F32 = jnp.float32
BF16 = jnp.bfloat16
I32 = jnp.int32
E = 128
REQ = 64
HALO = 5
OPPOSITE = (1, 0, 3, 2, 4)
G = 0.4


def derivative_table():
    points = [-1.0, -math.sqrt(3.0 / 7.0), 0.0, math.sqrt(3.0 / 7.0), 1.0]
    barycentric = []
    for i in range(5):
        product_value = 1.0
        for j in range(5):
            if j != i:
                product_value = product_value * (points[i] - points[j])
        barycentric.append(1.0 / product_value)
    matrix_values = np.zeros((5, 5))
    for i in range(5):
        for j in range(5):
            if j != i:
                matrix_values[i, j] = barycentric[j] / barycentric[i] / (points[i] - points[j])
        matrix_values[i, i] = -np.sum(matrix_values[i])
    return matrix_values


def face_node(face, a, b):
    edge = 0 if face % 2 == 0 else 4
    index = {0: (edge, a, b), 1: (a, edge, b), 2: (a, b, edge)}[face // 2]
    return 25 * index[0] + 5 * index[1] + index[2]


def oriented(orient, a, b):
    return {0: (a, b), 1: (b, a), 2: (4 - a, b), 3: (a, 4 - b)}[orient]


def split_table(table):
    high = table.astype(np.float32).astype(jnp.bfloat16)
    low = (table - high.astype(np.float64)).astype(np.float32).astype(jnp.bfloat16)
    return high, low


@functools.cache
def tables():
    d = derivative_table()
    eye = np.eye(5)
    ends = np.zeros((5, 5))
    ends[0, 0], ends[4, 4] = -0.5, 0.5
    along = [
        lambda m: np.kron(m, np.kron(eye, eye)),
        lambda m: np.kron(eye, np.kron(m, eye)),
        lambda m: np.kron(eye, np.kron(eye, m)),
    ]
    sweeps = np.zeros((512, 128))
    for axis in range(3):
        sweeps[128 * axis : 128 * axis + 125, :125] = along[axis](d.T + ends)
        sweeps[384:509, :125] += along[axis](d) @ along[axis](d.T)
    sweep_high, sweep_low = split_table(sweeps)
    traces = np.zeros((192, 128))
    to_nodes = np.zeros((3, 128, 128))
    turns = np.zeros((160, 512))
    penalties = np.zeros((512, 32))
    for face in range(6):
        axis, sign = face // 2, (1.0 if face % 2 else -1.0)
        for a in range(5):
            for b in range(5):
                node = face_node(face, a, b)
                traces[32 * face + 5 * a + b, node] = 1.0
                for term in range(3):
                    penalties[128 * axis + node, 8 * term + face] = 2.0 * sign
                    penalties[384 + node, 8 * term + face] = 1.0
                for term in range(2):
                    to_nodes[axis, node, 64 * term + 32 * (face % 2) + 5 * a + b] = 0.5 * sign
    dense = np.zeros((128, 160))
    for field in range(5):
        for ab in range(25):
            dense[25 * field + ab, 32 * field + ab] = 1.0
            for orient in range(4):
                oa, ob = oriented(orient, ab // 5, ab % 5)
                turns[32 * field + ab, 128 * orient + 25 * field + 5 * oa + ob] = 1.0
    as_bf16 = lambda t: t.astype(np.float32).astype(jnp.bfloat16)
    return (
        np.concatenate([sweep_high, sweep_low], 0),
        as_bf16(traces),
        as_bf16(to_nodes),
        as_bf16(penalties),
        as_bf16(dense),
        as_bf16(turns),
    )


def split(x):
    high = x.astype(BF16)
    return high, (x - high.astype(F32)).astype(BF16)


def mm(a, b):
    return lax.dot_general(a, b, (((1,), (0,)), ((), ())), preferred_element_type=F32)


def mm_nt(a, b):
    return lax.dot_general(a, b, (((1,), (1,)), ((), ())), preferred_element_type=F32)


def iota(shape, dim):
    return lax.broadcasted_iota(I32, shape, dim)


def one_if(condition):
    return jnp.where(condition, 1.0, 0.0)


def far_first(n):
    return sorted(range(1, n), key=lambda k: -min(k, n - k))


def whole(ref, sem):
    return pltpu.make_async_copy(ref, ref, sem)


def kernel(
    sizes,
    psi_hbm,
    obj_hbm,
    u_hbm,
    wp_hbm,
    metric_hbm,
    dt_hbm,
    visc_hbm,
    pen_hbm,
    fn_hbm,
    nf_hbm,
    fo_hbm,
    we_hbm,
    wf_hbm,
    od_hbm,
    os_hbm,
    sweeps_hbm,
    traces_hbm,
    to_nodes_hbm,
    penalties_hbm,
    dense_hbm,
    turns_hbm,
    adj_out,
    entries_ref,
    metric_ref,
    dt_ref,
    visc_ref,
    pen_ref,
    fn_ref,
    nf_ref,
    fo_ref,
    we_ref,
    wf_ref,
    od_ref,
    os_ref,
    sweeps_ref,
    traces_ref,
    to_nodes_ref,
    penalties_ref,
    dense_ref,
    turns_ref,
    psi,
    obj,
    u,
    wp,
    wpad,
    adj,
    psib,
    xp,
    xd,
    local_hot,
    request_hot,
    req_out,
    req_in,
    resp_out,
    resp_in,
    swept,
    pen_nodes,
    local_turned,
    near,
    far_masks,
    state,
    jump,
    wall_hot,
    owner_hot,
    send_a,
    recv_a,
    send_b,
    recv_b,
    in_sem,
    req_send_sem,
    req_recv_sem,
    resp_send_sem,
    resp_recv_sem,
    a_send_sem,
    a_recv_sem,
    b_send_sem,
    b_recv_sem,
    round2_sem,
    round3_sem,
    round4_sem,
):
    n_span, n_chord, n_wall = sizes
    n_plane = n_chord * n_wall
    s, c, w = (lax.axis_index(name) for name in AXES)
    part = (s * n_chord + c) * n_wall + w
    plane = c * n_wall + w

    def in_plane(k):
        there = jnp.bitwise_and(plane + k, n_plane - 1)
        return (s, lax.shift_right_arithmetic(there, n_wall.bit_length() - 1), jnp.bitwise_and(there, n_wall - 1))


    sources = {
        "fn": (fn_hbm, fn_ref),
        "nf": (nf_hbm, nf_ref),
        "psi": (psi_hbm, psi),
        "traces": (traces_hbm, traces_ref),
        "dense": (dense_hbm, dense_ref),
        "sweeps": (sweeps_hbm, sweeps_ref),
        "fo": (fo_hbm, fo_ref),
        "pen": (pen_hbm, pen_ref),
        "dt": (dt_hbm, dt_ref),
        "penalties": (penalties_hbm, penalties_ref),
        "we": (we_hbm, we_ref),
        "wf": (wf_hbm, wf_ref),
        "wp": (wp_hbm, wp),
        "od": (od_hbm, od_ref),
        "os": (os_hbm, os_ref),
        "turns": (turns_hbm, turns_ref),
        "to_nodes": (to_nodes_hbm, to_nodes_ref),
        "u": (u_hbm, u),
        "obj": (obj_hbm, obj),
        "metric": (metric_hbm, metric_ref),
        "visc": (visc_hbm, visc_ref),
    }
    loads = {}
    for i, (name, (src, dst)) in enumerate(sources.items()):
        loads[name] = pltpu.make_async_copy(src, dst, in_sem.at[i])
        loads[name].start()

    def ready(*names):
        for name in names:
            loads[name].wait()

    barrier = pltpu.get_barrier_semaphore()
    def along(ds, dc, other=False):
        return (
            jnp.bitwise_and(s + ds, n_span - 1),
            jnp.bitwise_and(c + dc, n_chord - 1),
            1 - w if other else w,
        )

    def greet(sem, near_chord):
        for peer in (
            along(1, 0),
            along(-1, 0),
            along(4, 0),
            along(-4, 0),
            along(0, near_chord),
            along(0, -near_chord),
            along(0, 0, True),
        ):
            pl.semaphore_signal(sem, inc=1, device_id=peer, device_id_type=MESH)

    greet(barrier, 1)

    ready("fn", "nf")
    fn, nf = fn_ref[...], nf_ref[...]
    offset = jnp.where(fn >= 0, lax.shift_right_arithmetic(fn, 7) - part, 1 << 20)
    elem = jnp.bitwise_and(fn, E - 1)
    slot = iota((8, E), 0)
    wanted = jnp.where(slot == 4, 1 - 2 * w, 1 << 21)
    for j, step in enumerate((-n_plane, n_plane, -n_wall, n_wall)):
        wanted = jnp.where(slot == j, step, wanted)
    named = [offset[f : f + 1] == wanted for f in range(6)]
    before = jnp.concatenate(
        [one_if(iota((E, E), 0) < iota((E, E), 1)), jnp.ones((E, E), F32)], 1
    ).astype(BF16)
    counts = mm(jnp.concatenate([one_if(m) for m in named], 0).astype(BF16), before)
    base = jnp.zeros((8, E), F32)
    place = iota((REQ, E), 0).astype(F32)
    sub16 = iota((16, E), 0)
    codes = []
    for f in range(6):
        rank = jnp.where(named[f], counts[8 * f : 8 * f + 8, :E] + base, -1.0)
        base = base + counts[8 * f : 8 * f + 8, E:]
        for j in range(HALO):
            request_hot[REQ * j : REQ * (j + 1), E * f : E * (f + 1)] = one_if(
                rank[j : j + 1] == place
            ).astype(BF16)
        code = jnp.where(
            sub16 == 0, elem[f : f + 1], jnp.where(sub16 == 1, nf[f : f + 1], (sub16 == 2).astype(I32))
        )
        codes.append(code.astype(F32).astype(BF16))
    codes = jnp.concatenate(codes, 1)
    for j in range(HALO):
        got = mm_nt(codes, request_hot[REQ * j : REQ * (j + 1), :])
        req_out[j] = jnp.zeros((1, E), F32)
        req_out[j, :, 0:REQ] = got[0:1] + 128.0 * got[1:2] + 2048.0 * (1.0 - got[2:3])

    pl.semaphore_wait(barrier, 7)
    beside = (along(-1, 0), along(1, 0), along(0, -1), along(0, 1), along(0, 0, True))
    requests = [
        pltpu.make_async_remote_copy(
            src_ref=req_out.at[j],
            dst_ref=req_in.at[OPPOSITE[j]],
            send_sem=req_send_sem,
            recv_sem=req_recv_sem,
            device_id=beside[j],
            device_id_type=MESH,
        )
        for j in range(HALO)
    ]
    for copy in requests:
        copy.start()
    greet(round2_sem, 1)

    ready("psi", "traces", "dense")
    for field in range(5):
        psib[0, 112:128, E * field : E * (field + 1)] = jnp.zeros((16, E), BF16)
        psib[1, 112:128, E * field : E * (field + 1)] = jnp.zeros((16, E), BF16)
        high, low = split(psi[field])
        psib[0, 0:125, E * field : E * (field + 1)] = high
        psib[1, 0:125, E * field : E * (field + 1)] = low
    for half in range(2):
        got = mm(traces_ref[...], psib[half]).astype(BF16)
        for field in range(5):
            for f in range(6):
                xp[160 * half + 32 * field : 160 * half + 32 * (field + 1), E * f : E * (f + 1)] = got[
                    32 * f : 32 * (f + 1), E * field : E * (field + 1)
                ]
        xd[128 * half : 128 * (half + 1), :] = mm(
            dense_ref[...], xp[160 * half : 160 * (half + 1), :]
        ).astype(BF16)

    slots8 = iota((8, E), 0)
    mine = jnp.full((8, E), -1, I32)
    for f in range(6):
        code = jnp.where(offset[f : f + 1] == 0, elem[f : f + 1] + E * nf[f : f + 1], -1)
        mine = jnp.where(slots8 == f, code, mine)
    ready("fo")
    fo = fo_ref[...]
    turned = jnp.concatenate(
        [mine.astype(F32), fo.astype(F32), jnp.zeros((E - 14, E), F32)], 0
    ).T
    columns = iota((E, 6 * E), 1).astype(F32)
    for f in range(6):
        local_hot[E * f : E * (f + 1), :] = one_if(turned[:, f : f + 1] == columns).astype(BF16)
    ready("sweeps", "pen", "penalties", "dt")
    swept[...] = (
        mm(sweeps_ref[0:512], psib[0]) + mm(sweeps_ref[512:1024], psib[0]) + mm(sweeps_ref[0:512], psib[1])
    )
    pen8 = jnp.concatenate([pen_ref[...], jnp.zeros((2, E), F32)], 0)
    pen_terms = []
    for _ in range(3):
        pen_high = pen8.astype(BF16).astype(F32)
        pen_terms.append(pen_high)
        pen8 = pen8 - pen_high
    pen_terms.append(jnp.zeros((8, E), F32))
    pen_nodes[...] = dt_ref[...] * mm(penalties_ref[...], jnp.concatenate(pen_terms, 0).astype(BF16))

    own_answers = mm_nt(local_hot[...], xd[...]).astype(BF16)
    for f in range(6):
        seen = jnp.broadcast_to(turned[:, 8 + f : 9 + f], (E, E))
        for o in range(4):
            mask = one_if(seen == o).astype(BF16)
            for half in range(2):
                local_turned[E * f : E * (f + 1), 512 * half + E * o : 512 * half + E * (o + 1)] = (
                    own_answers[E * f : E * (f + 1), E * half : E * (half + 1)] * mask
                )
    ready("turns")
    turns2 = jnp.concatenate([turns_ref[...], turns_ref[...]], 1)
    near[...] = mm_nt(turns2, local_turned[...])
    whole(req_in, req_recv_sem).wait()
    pl.semaphore_wait(round2_sem, 7)
    asked = jnp.zeros((8, E), F32)
    for j in range(HALO):
        asked = jnp.where(slots8 == j, req_in[j], asked)
    asked = jnp.concatenate([asked, jnp.zeros((E - 8, E), F32)], 0).T
    columns = iota((REQ, 6 * E), 1).astype(F32)
    for j in range(HALO):
        hot = one_if(asked[0:REQ, j : j + 1] == columns).astype(BF16)
        got = mm_nt(hot, xd[...])
        resp_out[j] = got[:, :E] + got[:, E:]
        copy = pltpu.make_async_remote_copy(
            src_ref=resp_out.at[j],
            dst_ref=resp_in.at[OPPOSITE[j]],
            send_sem=resp_send_sem,
            recv_sem=resp_recv_sem,
            device_id=beside[j],
            device_id_type=MESH,
        )
        copy.start()

    greet(round3_sem, 2)
    views = jnp.concatenate(
        [jnp.broadcast_to(fo[f : f + 1], (16, E)).astype(F32).astype(BF16) for f in range(6)], 1
    )
    views = mm_nt(request_hot[...], jnp.concatenate([views] * 8, 0))
    for o in range(4):
        far_masks[o] = one_if(views == o).astype(BF16)

    ready("we", "wf", "wp", "od", "os")
    wall_code = we_ref[...] + E * wf_ref[...]
    for g in range(6):
        wall_hot[E * g : E * (g + 1), :] = one_if(wall_code == iota((E, E), 0) + E * g).astype(BF16)
    for x in range(3):
        for field in range(5):
            wpad[x, field] = jnp.zeros((32, E), F32)
            wpad[x, field, 0:25] = wp[x, 25 * field : 25 * (field + 1)]
    owner = od_ref[...]
    owner_rows = jnp.broadcast_to(owner.astype(F32), (E, E))
    owner_columns = owner_rows.T
    earlier = one_if((owner_rows == owner_columns) & (iota((E, E), 1) < iota((E, E), 0)))
    rank = jnp.sum(earlier, axis=1, keepdims=True)
    owner_span = lax.shift_right_arithmetic(owner, n_plane.bit_length() - 1)
    owner_plane = jnp.bitwise_and(owner_columns.astype(I32), n_plane - 1).astype(F32)
    lane = iota((E, E), 1).astype(F32)
    for v in range(4):
        owner_hot[E * v : E * (v + 1), :] = one_if(lane == owner_plane + 16.0 * rank + 32.0 * v).astype(BF16)
    to_span = one_if(iota((16, E), 0) == owner_span)

    ready("u", "obj", "metric", "visc")
    metric, dt, visc = metric_ref[...], dt_ref[...], visc_ref[...]
    dt_metric, dt_visc = dt * metric, dt * visc

    def lanes(field):
        return slice(E * field, E * (field + 1))

    def transposed_flux(axes, vel, kinetic, enthalpy, weights):
        out = [0.0] * 5
        a_sum = 0.0
        for axis in axes:
            wd, vd = weights[axis], vel[axis]
            carried = wd[1] * vel[0] + wd[2] * vel[1] + wd[3] * vel[2] + enthalpy * wd[4]
            a_sum = a_sum + (wd[1 + axis] + vd * wd[4])
            out[0] = out[0] - vd * carried
            for i in range(3):
                out[1 + i] = out[1 + i] + vd * wd[1 + i]
            out[1 + axis] = out[1 + axis] + (wd[0] + carried)
            out[4] = out[4] + vd * wd[4]
        ga = G * a_sum
        out[0] = out[0] + kinetic * ga
        for i in range(3):
            out[1 + i] = out[1 + i] - vel[i] * ga
        out[4] = out[4] + ga
        return out

    for start in range(0, 125, 8):
        stop = min(start + 8, 125)
        cut = slice(start, stop)
        rho, m1, m2, m3, energy = (u[field, cut] for field in range(5))
        inverse = 1.0 / rho
        vel = (m1 * inverse, m2 * inverse, m3 * inverse)
        kinetic = 0.5 * (vel[0] * vel[0] + vel[1] * vel[1] + vel[2] * vel[2])
        pressure = G * (energy - rho * kinetic)
        enthalpy = (energy + pressure) * inverse
        for i, kept in enumerate((*vel, kinetic, enthalpy)):
            state[i, cut] = kept
        weights = [
            [swept[128 * axis + start : 128 * axis + stop, lanes(field)] for field in range(5)]
            for axis in range(3)
        ]
        out = transposed_flux(range(3), vel, kinetic, enthalpy, weights)
        pen = 1.0 - pen_nodes[384 + start : 384 + stop]
        for field in range(5):
            adj[field, cut] = (
                pen * psi[field, cut]
                + dt * obj[field, cut]
                - dt_metric * out[field]
                - dt_visc * swept[384 + start : 384 + stop, lanes(field)]
            )
    for field in range(5):
        adj[field, 125:128] = jnp.zeros((3, E), F32)
    ready("to_nodes")

    whole(resp_in, resp_recv_sem).wait()
    pl.semaphore_wait(round3_sem, 7)
    pl.semaphore_signal(round4_sem, inc=1, device_id=along(0, 0, True), device_id_type=MESH)
    answered = jnp.concatenate([resp_in[j] for j in range(HALO)], 0)
    answered = split(answered)
    placed = []
    for half in range(2):
        masked = jnp.concatenate([answered[half] * far_masks[o] for o in range(4)], 1)
        placed.append(mm_nt(turns_ref[...], masked).astype(BF16))
    far = mm(jnp.concatenate(placed, 0), request_hot[...])
    trace = split(near[...] + (far[:160] + far[160:]))
    for axis in range(3):
        rhs = jnp.concatenate(
            [
                jnp.concatenate(
                    [
                        trace[half][32 * field : 32 * (field + 1), E * f : E * (f + 1)]
                        for half in range(2)
                        for f in (2 * axis, 2 * axis + 1)
                    ],
                    0,
                )
                for field in range(5)
            ],
            1,
        )
        jump[axis] = mm(to_nodes_ref[axis], rhs)

    for start in range(0, 125, 8):
        stop = min(start + 8, 125)
        cut = slice(start, stop)
        axes = range(3) if start < 25 or stop > 100 else range(1, 3)
        vel = tuple(state[i, cut] for i in range(3))
        weights = [[jump[axis, cut, lanes(field)] for field in range(5)] for axis in range(3)]
        out = transposed_flux(axes, vel, state[3, cut], state[4, cut], weights)
        for field in range(5):
            new = adj[field, cut] - dt_metric * out[field]
            for axis in axes:
                new = new + pen_nodes[128 * axis + start : 128 * axis + stop] * weights[axis][field]
            adj[field, cut] = new
            adj_out[field, cut] = new

    for field in range(5):
        high, low = split(adj[field])
        psib[0, :, E * field : E * (field + 1)] = high
        psib[1, :, E * field : E * (field + 1)] = low
    for half in range(2):
        got = mm(traces_ref[...], psib[half]).astype(BF16)
        for field in range(5):
            for f in range(6):
                xp[160 * half + 32 * field : 160 * half + 32 * (field + 1), E * f : E * (f + 1)] = got[
                    32 * f : 32 * (f + 1), E * field : E * (field + 1)
                ]
    taken = mm(xp[...], wall_hot[...])
    taken = taken[:160] + taken[160:]
    values = [os_ref[...].astype(F32)]
    for x in range(3):
        total = wpad[x, 0] * taken[0:32]
        for field in range(1, 5):
            total = total + wpad[x, field] * taken[32 * field : 32 * (field + 1)]
        values.append(jnp.sum(total, axis=0, keepdims=True))
    spread = jnp.concatenate([to_span * value for value in values], 1)
    terms = []
    for _ in range(3):
        term = spread.astype(BF16)
        terms.append(term)
        spread = spread - term.astype(F32)
    sent = mm(jnp.concatenate(terms, 0), owner_hot[...])
    sent = sent[0:16] + sent[16:32] + sent[32:48]

    for k in range(n_span):
        send_a[k] = sent[k : k + 1]
    for k in far_first(n_span):
        there = jnp.bitwise_and(s + k, n_span - 1)
        pltpu.make_async_remote_copy(
            src_ref=send_a.at[there],
            dst_ref=recv_a.at[k],
            send_sem=a_send_sem,
            recv_sem=a_recv_sem,
            device_id=(there, c, w),
            device_id_type=MESH,
        ).start()
    recv_a[0] = send_a[s]
    whole(recv_a.at[1:n_span], a_recv_sem).wait()
    sub16 = iota((16, E), 0)
    arrived = jnp.zeros((16, E), F32)
    for k in range(n_span):
        arrived = jnp.where(sub16 == k, recv_a[k], arrived)
    arrived = jnp.concatenate([arrived, jnp.zeros((E - 16, E), F32)], 0).T
    onward = arrived[0:16]
    for i in range(1, 8):
        onward = onward + pltpu.roll(arrived[16 * i : 16 * (i + 1)], 16 * i, 1)
    for k in range(n_plane):
        send_b[k] = onward[k : k + 1]
    pl.semaphore_wait(round4_sem, 1)
    for k in far_first(n_plane):
        there = jnp.bitwise_and(plane + k, n_plane - 1)
        pltpu.make_async_remote_copy(
            src_ref=send_b.at[there],
            dst_ref=recv_b.at[k],
            send_sem=b_send_sem,
            recv_sem=b_recv_sem,
            device_id=in_plane(k),
            device_id_type=MESH,
        ).start()
    recv_b[0] = send_b[plane]
    whole(req_out, req_send_sem).wait()
    whole(resp_out, resp_send_sem).wait()
    whole(send_a.at[1:n_span], a_send_sem).wait()
    whole(recv_b.at[1:n_plane], b_recv_sem).wait()
    for k in range(n_plane):
        entries_ref[k : k + 1] = recv_b[k]
    whole(send_b.at[1:n_plane], b_send_sem).wait()


def finish(adj_from, entries_ref, adj_to, sens_to, sens, sems):
    copies = [
        pltpu.make_async_copy(adj_from.at[field], adj_to.at[field], sems.at[field]) for field in range(5)
    ]
    for copy in copies:
        copy.start()
    entries = entries_ref[...]
    slots = jnp.where(iota(entries.shape, 1) < 32, entries, 0.0)
    slots = slots + pltpu.roll(slots, 32, 1)
    slots = slots + pltpu.roll(slots, 64, 1)
    design = iota((E, E), 0).astype(F32)
    total = jnp.zeros((E, E), F32)
    for k in range(entries.shape[0]):
        total = total + jnp.where(slots[k : k + 1] == design, entries[k : k + 1], 0.0)
    terms = []
    for _ in range(3):
        term = total.astype(BF16)
        terms.append(term)
        total = total - term.astype(F32)
    coordinate = one_if(lax.shift_right_arithmetic(iota((16, E), 1), 5) == iota((16, E), 0) + 1).astype(BF16)
    sens[...] = mm_nt(jnp.concatenate([coordinate] * 3, 1), jnp.concatenate(terms, 1))[0:3]
    copies.append(pltpu.make_async_copy(sens, sens_to, sems.at[5]))
    copies[5].start()
    for copy in copies:
        copy.wait()


def on_device(sizes, *args):
    (psi, obj, u, metric, dt, visc, pen, fn, nf, fo, we, wf, wp, od, os_) = args
    row = lambda x: x.reshape(1, E)
    vmem = pl.BlockSpec(memory_space=pltpu.VMEM)
    hbm = pl.BlockSpec(memory_space=pltpu.HBM)
    n_span, n_chord, n_wall = sizes
    n_plane = n_chord * n_wall
    consts = tuple(jnp.asarray(t) for t in tables())
    results = pl.pallas_call(
        functools.partial(kernel, sizes),
        out_shape=(pltpu.VMEM((5, 125, E), F32), pltpu.VMEM((n_plane, E), F32)),
        in_specs=[hbm] * (15 + len(consts)),
        out_specs=(vmem, vmem),
        scratch_shapes=[
            *[pltpu.VMEM((1, E), F32)] * 3,
            pltpu.VMEM((6, E), F32),
            *[pltpu.VMEM((6, E), I32)] * 3,
            *[pltpu.VMEM((1, E), I32)] * 4,
            *[pltpu.VMEM(t.shape, BF16) for t in consts],
            pltpu.VMEM((5, 125, E), F32),
            pltpu.VMEM((5, 125, E), F32),
            pltpu.VMEM((5, 125, E), F32),
            pltpu.VMEM((3, 125, E), F32),
            pltpu.VMEM((3, 5, 32, E), F32),
            pltpu.VMEM((5, 128, E), F32),
            pltpu.VMEM((2, 128, 5 * E), BF16),
            pltpu.VMEM((320, 6 * E), BF16),
            pltpu.VMEM((256, 6 * E), BF16),
            pltpu.VMEM((6 * E, 6 * E), BF16),
            pltpu.VMEM((HALO * REQ, 6 * E), BF16),
            pltpu.VMEM((HALO, 1, E), F32),
            pltpu.VMEM((HALO, 1, E), F32),
            pltpu.VMEM((HALO, REQ, E), F32),
            pltpu.VMEM((HALO, REQ, E), F32),
            pltpu.VMEM((512, 5 * E), F32),
            pltpu.VMEM((512, E), F32),
            pltpu.VMEM((6 * E, 1024), BF16),
            pltpu.VMEM((160, 6 * E), F32),
            pltpu.VMEM((4, HALO * REQ, E), BF16),
            pltpu.VMEM((5, 128, E), F32),
            pltpu.VMEM((3, 128, 5 * E), F32),
            pltpu.VMEM((6 * E, E), BF16),
            pltpu.VMEM((4 * E, E), BF16),
            pltpu.VMEM((n_span, 1, E), F32),
            pltpu.VMEM((n_span, 1, E), F32),
            pltpu.VMEM((n_plane, 1, E), F32),
            pltpu.VMEM((n_plane, 1, E), F32),
            pltpu.SemaphoreType.DMA((15 + len(consts),)),
            *[pltpu.SemaphoreType.DMA] * 8,
            *[pltpu.SemaphoreType.REGULAR] * 3,
        ],
        compiler_params=pltpu.CompilerParams(
            collective_id=0, has_side_effects=True, vmem_limit_bytes=58 * 2**20
        ),
        name="adjoint_step",
    )(
        psi,
        obj,
        u,
        wp,
        row(metric),
        row(dt),
        row(visc),
        pen,
        fn,
        nf,
        fo,
        row(we),
        row(wf),
        row(od),
        row(os_),
        *consts,
    )
    return pl.pallas_call(
        finish,
        out_shape=(jax.ShapeDtypeStruct((5, 125, E), F32), jax.ShapeDtypeStruct((3, E), F32)),
        in_specs=[vmem] * 2,
        out_specs=(hbm, hbm),
        scratch_shapes=[pltpu.VMEM((3, E), F32), pltpu.SemaphoreType.DMA((6,))],
        compiler_params=pltpu.CompilerParams(vmem_limit_bytes=16 * 2**20),
        name="results",
    )(*results)


def solution(mesh):
    whole = P(None, None, AXES)
    plane = P(None, AXES)
    line = P(AXES)
    in_specs = (
        (whole,) * 3 + (line,) * 3 + (plane,) * 4 + (line,) * 2 + (whole, P(AXES, None), line)
    )
    sizes = tuple(mesh.shape[name] for name in AXES)
    return jax.shard_map(
        functools.partial(on_device, sizes),
        mesh=mesh,
        in_specs=in_specs,
        out_specs=(whole, plane),
        check_vma=False,
    )
```

time: 36.9 us -> 31.4 us (0.85)
  Pallas kernels: 33.9 us -> 30.7 us
  local copies, waits for them, and re-layouts: 2.3 us -> 0 us
    pallas_call x1 -> x2, Pallas kernels: 33.9 us -> 30.7 us  [the longest x1 29.7 us: on_device(): pl.pallas_call(functools.partial(kernel, sizes), out_shape=(pltpu.VMEM((5...]
    unnamed x4 -> x0, local copies, waits for them, and re-layouts: 2.3 us -> none
where the time goes in v2:
time: 31.4 us; the launch traced here: 31.3 us
  Pallas kernels  30.7 us (98%)
  between operations  0.64 us (2%)
    pallas_call x1, Pallas kernels, on_device(): pl.pallas_call(functools.partial(kernel, sizes), out_shape=(pltpu.VMEM((5...  29.7 us
    pallas_call x1, Pallas kernels, on_device(): pl.pallas_call(finish, out_shape=(jax.ShapeDtypeStruct((5, 125, E), F32),...  1 us

profile of v2, /device:TPU:1, one launch (start us, length us, event | category | flops | bytes accessed | tf_op | source)
XLA Modules:
  0.0 31.3 jit_solution(10525530071253334413)
XLA Ops:
  0.6 29.7 %adjoint_step.1 = (f32[5,125,128]{2,1,0:T(8,128)S(1)}, f32[16,128]{1,0:T(8,128)S(1)}) custom-call(f32[5,125,128]{2,1,0:T(8,128)} %psi_hbm.1, f32[5,125,128]{2,1,0:T(8,128)} %obj_hbm.1, f32[5,125,128]{2,1,0:T(8,128)} %u_hbm.1, f32[3,125,128]{2,1,0:T(8,128)} %wp_hbm.1, f32[1,128]{1,0:T(1,128)} %bitcast.7, f32[1,128]{1,0:T(1,128)} %bitcast.8, ...), custom_call_target="tpu_custom_call" | custom-call | tf_op jit(solution)/shard_map/adjoint_step/pallas_call | solution.py:644
  30.3 1.0 %results.1 = (f32[5,125,128]{2,1,0:T(8,128)}, f32[3,128]{1,0:T(4,128)}) custom-call(f32[5,125,128]{2,1,0:T(8,128)S(1)} %get-tuple-element.4.adj_from, f32[16,128]{1,0:T(8,128)S(1)} %get-tuple-element.5.entries_ref), custom_call_target="tpu_custom_call" | custom-call | tf_op jit(solution)/shard_map/results/pallas_call | solution.py:709

commit v3 on v2

--- a/solution.py
+++ b/solution.py
@@ -125,8 +125,14 @@
     return jnp.where(condition, 1.0, 0.0)
 
 
-def far_first(n):
-    return sorted(range(1, n), key=lambda k: -min(k, n - k))
+def ring_steps(k, n):
+    return min(k, n - k)
+
+
+def far_first(n_span, n_chord):
+    offsets = [(a, b) for a in range(n_span) for b in range(n_chord) if a or b]
+    steps = lambda o: ring_steps(o[0] // 4, 4) + ring_steps(o[0] % 4, 4) + ring_steps(o[1], n_chord)
+    return sorted(offsets, key=lambda o: -steps(o))
 
 
 def whole(ref, sem):
@@ -198,20 +204,23 @@
     state,
     jump,
     wall_hot,
-    owner_hot,
-    send_a,
-    recv_a,
-    send_b,
-    recv_b,
+    to_chip,
+    owner_out,
+    owner_in,
+    values_out,
+    values_in,
+    send_all,
     in_sem,
     req_send_sem,
     req_recv_sem,
     resp_send_sem,
     resp_recv_sem,
-    a_send_sem,
-    a_recv_sem,
-    b_send_sem,
-    b_recv_sem,
+    owner_send_sem,
+    owner_recv_sem,
+    values_send_sem,
+    values_recv_sem,
+    all_send_sem,
+    all_recv_sem,
     round2_sem,
     round3_sem,
     round4_sem,
@@ -220,12 +229,6 @@
     n_plane = n_chord * n_wall
     s, c, w = (lax.axis_index(name) for name in AXES)
     part = (s * n_chord + c) * n_wall + w
-    plane = c * n_wall + w
-
-    def in_plane(k):
-        there = jnp.bitwise_and(plane + k, n_plane - 1)
-        return (s, lax.shift_right_arithmetic(there, n_wall.bit_length() - 1), jnp.bitwise_and(there, n_wall - 1))
-
 
     sources = {
         "fn": (fn_hbm, fn_ref),
@@ -233,6 +236,7 @@
         "psi": (psi_hbm, psi),
         "traces": (traces_hbm, traces_ref),
         "dense": (dense_hbm, dense_ref),
+        "od": (od_hbm, od_ref),
         "sweeps": (sweeps_hbm, sweeps_ref),
         "fo": (fo_hbm, fo_ref),
         "pen": (pen_hbm, pen_ref),
@@ -241,7 +245,6 @@
         "we": (we_hbm, we_ref),
         "wf": (wf_hbm, wf_ref),
         "wp": (wp_hbm, wp),
-        "od": (od_hbm, od_ref),
         "os": (os_hbm, os_ref),
         "turns": (turns_hbm, turns_ref),
         "to_nodes": (to_nodes_hbm, to_nodes_ref),
@@ -253,6 +256,8 @@
     loads = {}
     for i, (name, (src, dst)) in enumerate(sources.items()):
         loads[name] = pltpu.make_async_copy(src, dst, in_sem.at[i])
+    first = ("fn", "nf", "psi", "traces", "dense")
+    for name in first:
         loads[name].start()
 
     def ready(*names):
@@ -267,19 +272,16 @@
             1 - w if other else w,
         )
 
-    def greet(sem, near_chord):
-        for peer in (
-            along(1, 0),
-            along(-1, 0),
-            along(4, 0),
-            along(-4, 0),
-            along(0, near_chord),
-            along(0, -near_chord),
-            along(0, 0, True),
-        ):
+    nearest = (along(1, 0), along(-1, 0), along(4, 0), along(-4, 0), along(0, 1), along(0, -1), along(0, 0, True))
+
+    def greet(sem, peers):
+        for peer in peers:
             pl.semaphore_signal(sem, inc=1, device_id=peer, device_id_type=MESH)
 
-    greet(barrier, 1)
+    greet(barrier, nearest)
+    for name in sources:
+        if name not in first:
+            loads[name].start()
 
     ready("fn", "nf")
     fn, nf = fn_ref[...], nf_ref[...]
@@ -330,7 +332,19 @@
     ]
     for copy in requests:
         copy.start()
-    greet(round2_sem, 1)
+    greet(round2_sem, nearest)
+    ready("od")
+    owner = od_ref[...]
+    owner_out[...] = owner.astype(F32)
+    owner_copy = pltpu.make_async_remote_copy(
+        src_ref=owner_out,
+        dst_ref=owner_in,
+        send_sem=owner_send_sem,
+        recv_sem=owner_recv_sem,
+        device_id=beside[4],
+        device_id_type=MESH,
+    )
+    owner_copy.start()
 
     ready("psi", "traces", "dense")
     for field in range(5):
@@ -390,6 +404,7 @@
     near[...] = mm_nt(turns2, local_turned[...])
     whole(req_in, req_recv_sem).wait()
     pl.semaphore_wait(round2_sem, 7)
+    greet(round3_sem, (along(0, 1), along(0, -1), along(5, 0), along(-5, 0)))
     asked = jnp.zeros((8, E), F32)
     for j in range(HALO):
         asked = jnp.where(slots8 == j, req_in[j], asked)
@@ -409,7 +424,6 @@
         )
         copy.start()
 
-    greet(round3_sem, 2)
     views = jnp.concatenate(
         [jnp.broadcast_to(fo[f : f + 1], (16, E)).astype(F32).astype(BF16) for f in range(6)], 1
     )
@@ -417,7 +431,7 @@
     for o in range(4):
         far_masks[o] = one_if(views == o).astype(BF16)
 
-    ready("we", "wf", "wp", "od", "os")
+    ready("we", "wf", "wp", "os")
     wall_code = we_ref[...] + E * wf_ref[...]
     for g in range(6):
         wall_hot[E * g : E * (g + 1), :] = one_if(wall_code == iota((E, E), 0) + E * g).astype(BF16)
@@ -425,18 +439,17 @@
         for field in range(5):
             wpad[x, field] = jnp.zeros((32, E), F32)
             wpad[x, field, 0:25] = wp[x, 25 * field : 25 * (field + 1)]
-    owner = od_ref[...]
     owner_rows = jnp.broadcast_to(owner.astype(F32), (E, E))
-    owner_columns = owner_rows.T
-    earlier = one_if((owner_rows == owner_columns) & (iota((E, E), 1) < iota((E, E), 0)))
-    rank = jnp.sum(earlier, axis=1, keepdims=True)
-    owner_span = lax.shift_right_arithmetic(owner, n_plane.bit_length() - 1)
-    owner_plane = jnp.bitwise_and(owner_columns.astype(I32), n_plane - 1).astype(F32)
-    lane = iota((E, E), 1).astype(F32)
-    for v in range(4):
-        owner_hot[E * v : E * (v + 1), :] = one_if(lane == owner_plane + 16.0 * rank + 32.0 * v).astype(BF16)
-    to_span = one_if(iota((16, E), 0) == owner_span)
-
+    earlier = one_if((owner_rows == owner_rows.T) & (iota((E, E), 0) < iota((E, E), 1)))
+    rank = jnp.sum(earlier, axis=0, keepdims=True)
+    owner_copy.wait_recv()
+    for half, named_owner in enumerate((owner, owner_in[...].astype(I32))):
+        chip = lax.shift_right_arithmetic(named_owner, n_wall.bit_length() - 1)
+        here = jnp.bitwise_and(named_owner, n_wall - 1) == w
+        to_chip[:, E * half : E * (half + 1)] = one_if(jnp.where(here, chip, -1) == iota((E, E), 0)).astype(BF16)
+
+    pl.semaphore_wait(round3_sem, 4)
+    greet(round4_sem, (along(0, 3), along(0, -3)))
     ready("u", "obj", "metric", "visc")
     metric, dt, visc = metric_ref[...], dt_ref[...], visc_ref[...]
     dt_metric, dt_visc = dt * metric, dt * visc
@@ -492,8 +505,6 @@
     ready("to_nodes")
 
     whole(resp_in, resp_recv_sem).wait()
-    pl.semaphore_wait(round3_sem, 7)
-    pl.semaphore_signal(round4_sem, inc=1, device_id=along(0, 0, True), device_id_type=MESH)
     answered = jnp.concatenate([resp_in[j] for j in range(HALO)], 0)
     answered = split(answered)
     placed = []
@@ -552,58 +563,50 @@
         for field in range(1, 5):
             total = total + wpad[x, field] * taken[32 * field : 32 * (field + 1)]
         values.append(jnp.sum(total, axis=0, keepdims=True))
-    spread = jnp.concatenate([to_span * value for value in values], 1)
+    mine = jnp.concatenate(values + values, 0)
+    mine = jnp.where(rank == lax.shift_right_arithmetic(slots8, 2).astype(F32), mine, 0.0)
+    values_out[...] = mine
+    values_copy = pltpu.make_async_remote_copy(
+        src_ref=values_out,
+        dst_ref=values_in,
+        send_sem=values_send_sem,
+        recv_sem=values_recv_sem,
+        device_id=beside[4],
+        device_id_type=MESH,
+    )
+    values_copy.start()
+    nothing = jnp.zeros((8, E), F32)
+    rest = jnp.zeros((E - 16, 2 * E), BF16)
+    values_copy.wait_recv()
+    both = jnp.concatenate(
+        [jnp.concatenate([mine, nothing], 0), jnp.concatenate([nothing, values_in[...]], 0)], 1
+    )
     terms = []
     for _ in range(3):
-        term = spread.astype(BF16)
-        terms.append(term)
-        spread = spread - term.astype(F32)
-    sent = mm(jnp.concatenate(terms, 0), owner_hot[...])
-    sent = sent[0:16] + sent[16:32] + sent[32:48]
-
-    for k in range(n_span):
-        send_a[k] = sent[k : k + 1]
-    for k in far_first(n_span):
-        there = jnp.bitwise_and(s + k, n_span - 1)
+        term = both.astype(BF16)
+        terms.append(jnp.concatenate([term, rest], 0))
+        both = both - term.astype(F32)
+    sent = mm_nt(jnp.concatenate([to_chip[...]] * 3, 1), jnp.concatenate(terms, 1))
+    for k in range(n_span * n_chord):
+        send_all[k] = sent[k : k + 1]
+    pl.semaphore_wait(round4_sem, 2)
+    for k, (ds, dc) in enumerate(far_first(n_span, n_chord)):
+        there = along(ds, dc)
         pltpu.make_async_remote_copy(
-            src_ref=send_a.at[there],
-            dst_ref=recv_a.at[k],
-            send_sem=a_send_sem,
-            recv_sem=a_recv_sem,
-            device_id=(there, c, w),
+            src_ref=send_all.at[there[0] * n_chord + there[1]],
+            dst_ref=entries_ref.at[k + 1],
+            send_sem=all_send_sem,
+            recv_sem=all_recv_sem,
+            device_id=there,
             device_id_type=MESH,
         ).start()
-    recv_a[0] = send_a[s]
-    whole(recv_a.at[1:n_span], a_recv_sem).wait()
-    sub16 = iota((16, E), 0)
-    arrived = jnp.zeros((16, E), F32)
-    for k in range(n_span):
-        arrived = jnp.where(sub16 == k, recv_a[k], arrived)
-    arrived = jnp.concatenate([arrived, jnp.zeros((E - 16, E), F32)], 0).T
-    onward = arrived[0:16]
-    for i in range(1, 8):
-        onward = onward + pltpu.roll(arrived[16 * i : 16 * (i + 1)], 16 * i, 1)
-    for k in range(n_plane):
-        send_b[k] = onward[k : k + 1]
-    pl.semaphore_wait(round4_sem, 1)
-    for k in far_first(n_plane):
-        there = jnp.bitwise_and(plane + k, n_plane - 1)
-        pltpu.make_async_remote_copy(
-            src_ref=send_b.at[there],
-            dst_ref=recv_b.at[k],
-            send_sem=b_send_sem,
-            recv_sem=b_recv_sem,
-            device_id=in_plane(k),
-            device_id_type=MESH,
-        ).start()
-    recv_b[0] = send_b[plane]
+    entries_ref[0] = send_all[s * n_chord + c]
     whole(req_out, req_send_sem).wait()
     whole(resp_out, resp_send_sem).wait()
-    whole(send_a.at[1:n_span], a_send_sem).wait()
-    whole(recv_b.at[1:n_plane], b_recv_sem).wait()
-    for k in range(n_plane):
-        entries_ref[k : k + 1] = recv_b[k]
-    whole(send_b.at[1:n_plane], b_send_sem).wait()
+    owner_copy.wait_send()
+    values_copy.wait_send()
+    whole(entries_ref.at[1 : n_span * n_chord], all_recv_sem).wait()
+    whole(send_all.at[1 : n_span * n_chord], all_send_sem).wait()
 
 
 def finish(adj_from, entries_ref, adj_to, sens_to, sens, sems):
@@ -612,21 +615,27 @@
     ]
     for copy in copies:
         copy.start()
-    entries = entries_ref[...]
-    slots = jnp.where(iota(entries.shape, 1) < 32, entries, 0.0)
-    slots = slots + pltpu.roll(slots, 32, 1)
-    slots = slots + pltpu.roll(slots, 64, 1)
+    entries = entries_ref[...].reshape(entries_ref.shape[0], E)
+    if entries.shape[0] < E:
+        entries = jnp.concatenate([entries, jnp.zeros((E - entries.shape[0], E), F32)], 0)
+    entries = entries.T
     design = iota((E, E), 0).astype(F32)
-    total = jnp.zeros((E, E), F32)
-    for k in range(entries.shape[0]):
-        total = total + jnp.where(slots[k : k + 1] == design, entries[k : k + 1], 0.0)
+    both = jnp.concatenate([entries[0:8], entries[8:16]], 1)
     terms = []
     for _ in range(3):
-        term = total.astype(BF16)
+        term = both.astype(BF16).astype(F32)
         terms.append(term)
-        total = total - term.astype(F32)
-    coordinate = one_if(lax.shift_right_arithmetic(iota((16, E), 1), 5) == iota((16, E), 0) + 1).astype(BF16)
-    sens[...] = mm_nt(jnp.concatenate([coordinate] * 3, 1), jnp.concatenate(terms, 1))[0:3]
+        both = both - term
+    terms = jnp.concatenate(terms, 0).astype(BF16)
+    total = jnp.zeros((3, E), F32)
+    for r in range(2):
+        hot = jnp.concatenate(
+            [one_if(entries[8 * g + 4 * r : 8 * g + 4 * r + 1] == design).astype(BF16) for g in range(2)], 1
+        )
+        got = mm_nt(terms, hot)
+        got = got[0:8] + got[8:16] + got[16:24]
+        total = total + got[4 * r + 1 : 4 * r + 4]
+    sens[...] = total
     copies.append(pltpu.make_async_copy(sens, sens_to, sems.at[5]))
     copies[5].start()
     for copy in copies:
@@ -639,11 +648,11 @@
     vmem = pl.BlockSpec(memory_space=pltpu.VMEM)
     hbm = pl.BlockSpec(memory_space=pltpu.HBM)
     n_span, n_chord, n_wall = sizes
-    n_plane = n_chord * n_wall
+    n_chips = n_span * n_chord
     consts = tuple(jnp.asarray(t) for t in tables())
     results = pl.pallas_call(
         functools.partial(kernel, sizes),
-        out_shape=(pltpu.VMEM((5, 125, E), F32), pltpu.VMEM((n_plane, E), F32)),
+        out_shape=(pltpu.VMEM((5, 125, E), F32), pltpu.VMEM((n_chips, 1, E), F32)),
         in_specs=[hbm] * (15 + len(consts)),
         out_specs=(vmem, vmem),
         scratch_shapes=[
@@ -675,13 +684,14 @@
             pltpu.VMEM((5, 128, E), F32),
             pltpu.VMEM((3, 128, 5 * E), F32),
             pltpu.VMEM((6 * E, E), BF16),
-            pltpu.VMEM((4 * E, E), BF16),
-            pltpu.VMEM((n_span, 1, E), F32),
-            pltpu.VMEM((n_span, 1, E), F32),
-            pltpu.VMEM((n_plane, 1, E), F32),
-            pltpu.VMEM((n_plane, 1, E), F32),
+            pltpu.VMEM((E, 2 * E), BF16),
+            pltpu.VMEM((1, E), F32),
+            pltpu.VMEM((1, E), F32),
+            pltpu.VMEM((8, E), F32),
+            pltpu.VMEM((8, E), F32),
+            pltpu.VMEM((n_chips, 1, E), F32),
             pltpu.SemaphoreType.DMA((15 + len(consts),)),
-            *[pltpu.SemaphoreType.DMA] * 8,
+            *[pltpu.SemaphoreType.DMA] * 10,
             *[pltpu.SemaphoreType.REGULAR] * 3,
         ],
         compiler_params=pltpu.CompilerParams(

time: 31.4 us -> 29.7 us (0.946)
  Pallas kernels: 30.7 us -> 28.9 us
    pallas_call x1, Pallas kernels: 29.7 us -> 28.1 us  [on_device(): pl.pallas_call(functools.partial(kernel, sizes), out_shape=(pltpu.VMEM((5...]
where the time goes in v3:
time: 29.7 us; the launch traced here: 29.6 us
  Pallas kernels  28.9 us (97%)
  between operations  0.64 us (2%)
    pallas_call x1, Pallas kernels, on_device(): pl.pallas_call(functools.partial(kernel, sizes), out_shape=(pltpu.VMEM((5...  28.1 us
    pallas_call x1, Pallas kernels, on_device(): pl.pallas_call(finish, out_shape=(jax.ShapeDtypeStruct((5, 125, E), F32),...  0.85 us

profile of v3, /device:TPU:1, one launch (start us, length us, event | category | flops | bytes accessed | tf_op | source)
XLA Modules:
  0.0 29.6 jit_solution(12584546993976593701)
XLA Ops:
  0.6 28.1 %adjoint_step.1 = (f32[5,125,128]{2,1,0:T(8,128)S(1)}, f32[128,1,128]{2,1,0:T(1,128)S(1)}) custom-call(f32[5,125,128]{2,1,0:T(8,128)} %psi_hbm.1, f32[5,125,128]{2,1,0:T(8,128)} %obj_hbm.1, f32[5,125,128]{2,1,0:T(8,128)} %u_hbm.1, f32[3,125,128]{2,1,0:T(8,128)} %wp_hbm.1, f32[1,128]{1,0:T(1,128)} %bitcast.7, f32[1,128]{1,0:T(1,128)} %bitcast.8, ...), custom_call_target="tpu_custom_call" | custom-call | tf_op jit(solution)/shard_map/adjoint_step/pallas_call | solution.py:653
  28.7 0.8 %results.1 = (f32[5,125,128]{2,1,0:T(8,128)}, f32[3,128]{1,0:T(4,128)}) custom-call(f32[5,125,128]{2,1,0:T(8,128)S(1)} %get-tuple-element.4.adj_from, f32[128,1,128]{2,1,0:T(1,128)S(1)} %get-tuple-element.5.entries_ref), custom_call_target="tpu_custom_call" | custom-call | tf_op jit(solution)/shard_map/results/pallas_call | solution.py:719

commit v4 on v3

--- a/solution.py
+++ b/solution.py
@@ -1,4 +1,5 @@
 import functools
+import itertools
 import math
 
 import jax
@@ -129,9 +130,12 @@
     return min(k, n - k)
 
 
-def far_first(n_span, n_chord):
-    offsets = [(a, b) for a in range(n_span) for b in range(n_chord) if a or b]
-    steps = lambda o: ring_steps(o[0] // 4, 4) + ring_steps(o[0] % 4, 4) + ring_steps(o[1], n_chord)
+def far_first(n_span, n_chord, n_wall):
+    rows = max(n_span // 4, 1)
+    wide = n_span // rows
+    sizes = (rows, wide, n_chord, n_wall)
+    offsets = [o for o in itertools.product(*map(range, sizes)) if any(o)]
+    steps = lambda o: sum(ring_steps(k, n) for k, n in zip(o[:3], sizes)) + 0.1 * o[3]
     return sorted(offsets, key=lambda o: -steps(o))
 
 
@@ -204,21 +208,13 @@
     state,
     jump,
     wall_hot,
-    to_chip,
-    owner_out,
-    owner_in,
-    values_out,
-    values_in,
+    to_owner,
     send_all,
     in_sem,
     req_send_sem,
     req_recv_sem,
     resp_send_sem,
     resp_recv_sem,
-    owner_send_sem,
-    owner_recv_sem,
-    values_send_sem,
-    values_recv_sem,
     all_send_sem,
     all_recv_sem,
     round2_sem,
@@ -333,19 +329,6 @@
     for copy in requests:
         copy.start()
     greet(round2_sem, nearest)
-    ready("od")
-    owner = od_ref[...]
-    owner_out[...] = owner.astype(F32)
-    owner_copy = pltpu.make_async_remote_copy(
-        src_ref=owner_out,
-        dst_ref=owner_in,
-        send_sem=owner_send_sem,
-        recv_sem=owner_recv_sem,
-        device_id=beside[4],
-        device_id_type=MESH,
-    )
-    owner_copy.start()
-
     ready("psi", "traces", "dense")
     for field in range(5):
         psib[0, 112:128, E * field : E * (field + 1)] = jnp.zeros((16, E), BF16)
@@ -390,48 +373,51 @@
     pen_terms.append(jnp.zeros((8, E), F32))
     pen_nodes[...] = dt_ref[...] * mm(penalties_ref[...], jnp.concatenate(pen_terms, 0).astype(BF16))
 
-    own_answers = mm_nt(local_hot[...], xd[...]).astype(BF16)
-    for f in range(6):
-        seen = jnp.broadcast_to(turned[:, 8 + f : 9 + f], (E, E))
-        for o in range(4):
-            mask = one_if(seen == o).astype(BF16)
-            for half in range(2):
-                local_turned[E * f : E * (f + 1), 512 * half + E * o : 512 * half + E * (o + 1)] = (
-                    own_answers[E * f : E * (f + 1), E * half : E * (half + 1)] * mask
-                )
-    ready("turns")
-    turns2 = jnp.concatenate([turns_ref[...], turns_ref[...]], 1)
-    near[...] = mm_nt(turns2, local_turned[...])
     whole(req_in, req_recv_sem).wait()
     pl.semaphore_wait(round2_sem, 7)
-    greet(round3_sem, (along(0, 1), along(0, -1), along(5, 0), along(-5, 0)))
+    greet(round3_sem, (along(0, 2), along(0, -2), along(8, 0)))
     asked = jnp.zeros((8, E), F32)
     for j in range(HALO):
         asked = jnp.where(slots8 == j, req_in[j], asked)
     asked = jnp.concatenate([asked, jnp.zeros((E - 8, E), F32)], 0).T
     columns = iota((REQ, 6 * E), 1).astype(F32)
+    hot = [one_if(asked[0:REQ, j : j + 1] == columns).astype(BF16) for j in range(HALO)]
+    answers = mm_nt(jnp.concatenate(hot, 0), xd[...])
     for j in range(HALO):
-        hot = one_if(asked[0:REQ, j : j + 1] == columns).astype(BF16)
-        got = mm_nt(hot, xd[...])
-        resp_out[j] = got[:, :E] + got[:, E:]
-        copy = pltpu.make_async_remote_copy(
+        resp_out[j] = answers[REQ * j : REQ * (j + 1), :E] + answers[REQ * j : REQ * (j + 1), E:]
+    for j in range(HALO):
+        pltpu.make_async_remote_copy(
             src_ref=resp_out.at[j],
             dst_ref=resp_in.at[OPPOSITE[j]],
             send_sem=resp_send_sem,
             recv_sem=resp_recv_sem,
             device_id=beside[j],
             device_id_type=MESH,
+        ).start()
+
+    @pl.when(s >= 0)
+    def _():
+        own_answers = mm_nt(local_hot[...], xd[...]).astype(BF16)
+        for f in range(6):
+            seen = jnp.broadcast_to(turned[:, 8 + f : 9 + f], (E, E))
+            for o in range(4):
+                mask = one_if(seen == o).astype(BF16)
+                for half in range(2):
+                    local_turned[E * f : E * (f + 1), 512 * half + E * o : 512 * half + E * (o + 1)] = (
+                        own_answers[E * f : E * (f + 1), E * half : E * (half + 1)] * mask
+                    )
+        ready("turns")
+        turns2 = jnp.concatenate([turns_ref[...], turns_ref[...]], 1)
+        near[...] = mm_nt(turns2, local_turned[...])
+        views = jnp.concatenate(
+            [jnp.broadcast_to(fo[f : f + 1], (16, E)).astype(F32).astype(BF16) for f in range(6)], 1
         )
-        copy.start()
-
-    views = jnp.concatenate(
-        [jnp.broadcast_to(fo[f : f + 1], (16, E)).astype(F32).astype(BF16) for f in range(6)], 1
-    )
-    views = mm_nt(request_hot[...], jnp.concatenate([views] * 8, 0))
-    for o in range(4):
-        far_masks[o] = one_if(views == o).astype(BF16)
-
-    ready("we", "wf", "wp", "os")
+        views = mm_nt(request_hot[...], jnp.concatenate([views] * 8, 0))
+        for o in range(4):
+            far_masks[o] = one_if(views == o).astype(BF16)
+
+    ready("we", "wf", "wp", "os", "od")
+    owner = od_ref[...]
     wall_code = we_ref[...] + E * wf_ref[...]
     for g in range(6):
         wall_hot[E * g : E * (g + 1), :] = one_if(wall_code == iota((E, E), 0) + E * g).astype(BF16)
@@ -442,14 +428,13 @@
     owner_rows = jnp.broadcast_to(owner.astype(F32), (E, E))
     earlier = one_if((owner_rows == owner_rows.T) & (iota((E, E), 0) < iota((E, E), 1)))
     rank = jnp.sum(earlier, axis=0, keepdims=True)
-    owner_copy.wait_recv()
-    for half, named_owner in enumerate((owner, owner_in[...].astype(I32))):
-        chip = lax.shift_right_arithmetic(named_owner, n_wall.bit_length() - 1)
-        here = jnp.bitwise_and(named_owner, n_wall - 1) == w
-        to_chip[:, E * half : E * (half + 1)] = one_if(jnp.where(here, chip, -1) == iota((E, E), 0)).astype(BF16)
-
-    pl.semaphore_wait(round3_sem, 4)
-    greet(round4_sem, (along(0, 3), along(0, -3)))
+    to_owner[...] = one_if(owner == iota((2 * E, E), 0)).astype(BF16)
+
+    pl.semaphore_wait(round3_sem, 3)
+    greet(
+        round4_sem,
+        (along(1, 2, True), along(-1, -2, True), along(8, 1), along(8, -1), along(6, 0), along(-6, 0)),
+    )
     ready("u", "obj", "metric", "visc")
     metric, dt, visc = metric_ref[...], dt_ref[...], visc_ref[...]
     dt_metric, dt_visc = dt * metric, dt * visc
@@ -507,12 +492,13 @@
     whole(resp_in, resp_recv_sem).wait()
     answered = jnp.concatenate([resp_in[j] for j in range(HALO)], 0)
     answered = split(answered)
-    placed = []
-    for half in range(2):
-        masked = jnp.concatenate([answered[half] * far_masks[o] for o in range(4)], 1)
-        placed.append(mm_nt(turns_ref[...], masked).astype(BF16))
-    far = mm(jnp.concatenate(placed, 0), request_hot[...])
-    trace = split(near[...] + (far[:160] + far[160:]))
+    masked = jnp.concatenate(
+        [jnp.concatenate([part * far_masks[o] for o in range(4)], 1) for part in answered], 0
+    )
+    placed = mm_nt(turns_ref[...], masked).astype(BF16)
+    far = mm(placed, jnp.concatenate([request_hot[...]] * 2, 0))
+    trace = split(near[...] + far)
+    jumps = []
     for axis in range(3):
         rhs = jnp.concatenate(
             [
@@ -528,14 +514,14 @@
             ],
             1,
         )
-        jump[axis] = mm(to_nodes_ref[axis], rhs)
+        jumps.append(mm(to_nodes_ref[axis], rhs))
 
     for start in range(0, 125, 8):
         stop = min(start + 8, 125)
         cut = slice(start, stop)
         axes = range(3) if start < 25 or stop > 100 else range(1, 3)
         vel = tuple(state[i, cut] for i in range(3))
-        weights = [[jump[axis, cut, lanes(field)] for field in range(5)] for axis in range(3)]
+        weights = [[jumps[axis][cut, lanes(field)] for field in range(5)] for axis in range(3)]
         out = transposed_flux(axes, vel, state[3, cut], state[4, cut], weights)
         for field in range(5):
             new = adj[field, cut] - dt_metric * out[field]
@@ -565,48 +551,36 @@
         values.append(jnp.sum(total, axis=0, keepdims=True))
     mine = jnp.concatenate(values + values, 0)
     mine = jnp.where(rank == lax.shift_right_arithmetic(slots8, 2).astype(F32), mine, 0.0)
-    values_out[...] = mine
-    values_copy = pltpu.make_async_remote_copy(
-        src_ref=values_out,
-        dst_ref=values_in,
-        send_sem=values_send_sem,
-        recv_sem=values_recv_sem,
-        device_id=beside[4],
-        device_id_type=MESH,
-    )
-    values_copy.start()
-    nothing = jnp.zeros((8, E), F32)
-    rest = jnp.zeros((E - 16, 2 * E), BF16)
-    values_copy.wait_recv()
-    both = jnp.concatenate(
-        [jnp.concatenate([mine, nothing], 0), jnp.concatenate([nothing, values_in[...]], 0)], 1
-    )
+    nothing = jnp.zeros((E - 16, E), BF16)
     terms = []
     for _ in range(3):
-        term = both.astype(BF16)
-        terms.append(jnp.concatenate([term, rest], 0))
-        both = both - term.astype(F32)
-    sent = mm_nt(jnp.concatenate([to_chip[...]] * 3, 1), jnp.concatenate(terms, 1))
-    for k in range(n_span * n_chord):
+        term = mine.astype(BF16).astype(F32)
+        terms.append(jnp.concatenate([jnp.concatenate([term, jnp.zeros((8, E), F32)], 0).astype(BF16), nothing], 0))
+        mine = mine - term
+    sent = mm_nt(jnp.concatenate([to_owner[...]] * 3, 1), jnp.concatenate(terms, 1))
+    devices = n_span * n_chord * n_wall
+    for k in range(devices):
         send_all[k] = sent[k : k + 1]
-    pl.semaphore_wait(round4_sem, 2)
-    for k, (ds, dc) in enumerate(far_first(n_span, n_chord)):
-        there = along(ds, dc)
+    pl.semaphore_wait(round4_sem, 6)
+    wide = n_span // max(n_span // 4, 1)
+    for k, (dy, dx, dz, dw) in enumerate(far_first(n_span, n_chord, n_wall)):
+        x = jnp.bitwise_and(s + dx, wide - 1)
+        y = jnp.bitwise_and(s + wide * dy, n_span - wide)
+        z = jnp.bitwise_and(c + dz, n_chord - 1)
+        core = 1 - w if dw else w
         pltpu.make_async_remote_copy(
-            src_ref=send_all.at[there[0] * n_chord + there[1]],
+            src_ref=send_all.at[((y + x) * n_chord + z) * n_wall + core],
             dst_ref=entries_ref.at[k + 1],
             send_sem=all_send_sem,
             recv_sem=all_recv_sem,
-            device_id=there,
+            device_id=(y + x, z, core),
             device_id_type=MESH,
         ).start()
-    entries_ref[0] = send_all[s * n_chord + c]
+    entries_ref[0] = send_all[part]
     whole(req_out, req_send_sem).wait()
     whole(resp_out, resp_send_sem).wait()
-    owner_copy.wait_send()
-    values_copy.wait_send()
-    whole(entries_ref.at[1 : n_span * n_chord], all_recv_sem).wait()
-    whole(send_all.at[1 : n_span * n_chord], all_send_sem).wait()
+    whole(entries_ref.at[1:devices], all_recv_sem).wait()
+    whole(send_all.at[1:devices], all_send_sem).wait()
 
 
 def finish(adj_from, entries_ref, adj_to, sens_to, sens, sems):
@@ -616,11 +590,11 @@
     for copy in copies:
         copy.start()
     entries = entries_ref[...].reshape(entries_ref.shape[0], E)
-    if entries.shape[0] < E:
-        entries = jnp.concatenate([entries, jnp.zeros((E - entries.shape[0], E), F32)], 0)
-    entries = entries.T
+    if entries.shape[0] < 2 * E:
+        entries = jnp.concatenate([entries, jnp.zeros((2 * E - entries.shape[0], E), F32)], 0)
+    entries = [entries[E * g : E * (g + 1)].T for g in range(2)]
     design = iota((E, E), 0).astype(F32)
-    both = jnp.concatenate([entries[0:8], entries[8:16]], 1)
+    both = jnp.concatenate([e[0:8] for e in entries], 1)
     terms = []
     for _ in range(3):
         term = both.astype(BF16).astype(F32)
@@ -630,7 +604,7 @@
     total = jnp.zeros((3, E), F32)
     for r in range(2):
         hot = jnp.concatenate(
-            [one_if(entries[8 * g + 4 * r : 8 * g + 4 * r + 1] == design).astype(BF16) for g in range(2)], 1
+            [one_if(e[4 * r : 4 * r + 1] == design).astype(BF16) for e in entries], 1
         )
         got = mm_nt(terms, hot)
         got = got[0:8] + got[8:16] + got[16:24]
@@ -648,11 +622,11 @@
     vmem = pl.BlockSpec(memory_space=pltpu.VMEM)
     hbm = pl.BlockSpec(memory_space=pltpu.HBM)
     n_span, n_chord, n_wall = sizes
-    n_chips = n_span * n_chord
+    n_devices = n_span * n_chord * n_wall
     consts = tuple(jnp.asarray(t) for t in tables())
     results = pl.pallas_call(
         functools.partial(kernel, sizes),
-        out_shape=(pltpu.VMEM((5, 125, E), F32), pltpu.VMEM((n_chips, 1, E), F32)),
+        out_shape=(pltpu.VMEM((5, 125, E), F32), pltpu.VMEM((n_devices, 1, E), F32)),
         in_specs=[hbm] * (15 + len(consts)),
         out_specs=(vmem, vmem),
         scratch_shapes=[
@@ -684,14 +658,10 @@
             pltpu.VMEM((5, 128, E), F32),
             pltpu.VMEM((3, 128, 5 * E), F32),
             pltpu.VMEM((6 * E, E), BF16),
-            pltpu.VMEM((E, 2 * E), BF16),
-            pltpu.VMEM((1, E), F32),
-            pltpu.VMEM((1, E), F32),
-            pltpu.VMEM((8, E), F32),
-            pltpu.VMEM((8, E), F32),
-            pltpu.VMEM((n_chips, 1, E), F32),
+            pltpu.VMEM((2 * E, E), BF16),
+            pltpu.VMEM((n_devices, 1, E), F32),
             pltpu.SemaphoreType.DMA((15 + len(consts),)),
-            *[pltpu.SemaphoreType.DMA] * 10,
+            *[pltpu.SemaphoreType.DMA] * 6,
             *[pltpu.SemaphoreType.REGULAR] * 3,
         ],
         compiler_params=pltpu.CompilerParams(

time: 29.7 us -> 29.1 us (0.980)
  Pallas kernels: 28.9 us -> 28.3 us
    pallas_call x1, Pallas kernels: 28.1 us -> 27.4 us  [on_device(): pl.pallas_call(functools.partial(kernel, sizes), out_shape=(pltpu.VMEM((5...]
where the time goes in v4:
time: 29.1 us; the launch traced here: 29 us
  Pallas kernels  28.3 us (97%)
  between operations  0.64 us (2%)
    pallas_call x1, Pallas kernels, on_device(): pl.pallas_call(functools.partial(kernel, sizes), out_shape=(pltpu.VMEM((5...  27.4 us
    pallas_call x1, Pallas kernels, on_device(): pl.pallas_call(finish, out_shape=(jax.ShapeDtypeStruct((5, 125, E), F32),...  0.87 us

profile of v4, /device:TPU:1, one launch (start us, length us, event | category | flops | bytes accessed | tf_op | source)
XLA Modules:
  0.0 29.0 jit_solution(1296968869090978359)
XLA Ops:
  0.6 27.4 %adjoint_step.1 = (f32[5,125,128]{2,1,0:T(8,128)S(1)}, f32[256,1,128]{2,1,0:T(1,128)S(1)}) custom-call(f32[5,125,128]{2,1,0:T(8,128)} %psi_hbm.1, f32[5,125,128]{2,1,0:T(8,128)} %obj_hbm.1, f32[5,125,128]{2,1,0:T(8,128)} %u_hbm.1, f32[3,125,128]{2,1,0:T(8,128)} %wp_hbm.1, f32[1,128]{1,0:T(1,128)} %bitcast.7, f32[1,128]{1,0:T(1,128)} %bitcast.8, ...), custom_call_target="tpu_custom_call" | custom-call | tf_op jit(solution)/shard_map/adjoint_step/pallas_call | solution.py:627
  28.1 0.9 %results.1 = (f32[5,125,128]{2,1,0:T(8,128)}, f32[3,128]{1,0:T(4,128)}) custom-call(f32[5,125,128]{2,1,0:T(8,128)S(1)} %get-tuple-element.4.adj_from, f32[256,1,128]{2,1,0:T(1,128)S(1)} %get-tuple-element.5.entries_ref), custom_call_target="tpu_custom_call" | custom-call | tf_op jit(solution)/shard_map/results/pallas_call | solution.py:689
